TPU v7x, 512 devices: a whole 4x8x8 slice. The times are simulated.
512 devices in a mesh: tm: 2 (over core), space: 256 (over z, y, x).
Axes of the slice: x: 4, y: 8, z: 8, core: 2. Of those that a mesh axis runs over, the one named last changes fastest.
Arguments:
- initial_state: float32 [256, 320, 128], P('space'), may hold values from -6 to 6
- volume_block: float32 [320, 320], replicated, may hold values from -0.15625 to 0.15625
- face_blocks: float32 [6, 320, 80], replicated, may hold values from -0.125 to 0.125
- coarse_rate: float32 [320, 320], replicated, may hold values from -0.3125 to 0.3125
Outputs:
- start_states: float32 [4, 256, 320, 128], P('tm', 'space')
- fine_ends: float32 [4, 256, 320, 128], P('tm', 'space')
All inputs are finite; a program needn't handle non-finite values.
Results may differ from a plain program's by a relative error of at most 0.0001.
Values sent between devices are 32-bit elements; how exact they have to be, the bound alone decides.
No kernel may reach another device: no remote copies, remote signals or barrier semaphores. Data moves between devices by JAX's collectives and lax.ppermute only.
A program may use at most 64 MiB of HBM per device.

v0:
```python
import jax
import jax.numpy as jnp
from jax import lax
from jax.sharding import PartitionSpec as P

F = 5
ITERS = 2
ST_DEV = 2
EZ = 8


step_length = 0.25


def passed_along(block, axis, distance):
    devices = range(lax.axis_size(axis))
    route = [((i - distance) % len(devices), i) for i in devices]
    return lax.ppermute(block, axis, route)


def passed_along_2(shard, axis, by):
    devices = lax.axis_size(axis)
    pairs = [(i, i + by) for i in range(devices) if 0 <= i + by < devices]
    return lax.ppermute(shard, axis, pairs)


def face(state, which, level):
    lead = state.shape[:-2]
    cells = state.shape[-1]
    if which == 0:
        grid = state.reshape(lead + (F, 4, 16, cells))
    elif which == 1:
        grid = state.reshape(lead + (F * 4, 4, 4, cells))
    else:
        grid = state.reshape(lead + (F * 16, 4, cells))
    axis_at = len(lead) + 1 if which == 0 else len(lead) + 1 if which == 1 else len(lead) + 1
    if which == 1:
        axis_at = len(lead) + 1
    picked = lax.index_in_dim(grid, level, axis_at, keepdims=False)
    return picked.reshape(lead + (F * 16, cells))


def along_z(trace, step):
    cells = trace.shape[-1]
    column = lax.broadcasted_iota(jnp.int32, (cells,), 0) % EZ
    if step == 1:
        inside = jnp.roll(trace, 1, axis=-1)
        wrapped = jnp.roll(trace, -(EZ - 1), axis=-1)
        return jnp.where(column == 0, wrapped, inside)
    inside = jnp.roll(trace, -1, axis=-1)
    wrapped = jnp.roll(trace, EZ - 1, axis=-1)
    return jnp.where(column == EZ - 1, wrapped, inside)


def apply(block, field):
    return jnp.einsum("ab,...bq->...aq", block, field, precision=lax.Precision.HIGHEST)


def assemble(state, volume_block, face_blocks, minus_x, plus_x):
    minus_y = jnp.roll(face(state, 1, 3), EZ, axis=-1)
    plus_y = jnp.roll(face(state, 1, 0), -EZ, axis=-1)
    minus_z = along_z(face(state, 2, 3), 1)
    plus_z = along_z(face(state, 2, 0), -1)
    total = apply(volume_block, state) + apply(face_blocks[0], minus_x)
    total = total + apply(face_blocks[1], plus_x)
    total = total + apply(face_blocks[2], minus_y) + apply(face_blocks[3], plus_y)
    total = total + apply(face_blocks[4], minus_z) + apply(face_blocks[5], plus_z)
    return total


def evaluate(state, volume_block, face_blocks):
    upper = face(state, 0, 3)
    lower = face(state, 0, 0)
    below = passed_along(upper, "space", 1)
    above = passed_along(lower, "space", -1)
    minus_x = jnp.concatenate([below, upper[..., :-1, :, :]], axis=-3)
    plus_x = jnp.concatenate([lower[..., 1:, :, :], above], axis=-3)
    return assemble(state, volume_block, face_blocks, minus_x, plus_x)


def per_device(initial_state, volume_block, face_blocks, coarse_rate):
    position = lax.axis_index("tm")
    slices = lax.axis_size("tm")

    def coarse(value):
        return value + step_length * apply(coarse_rate, value)

    def local_chain(begin, correction):

        def advance(value, term):
            return (coarse(value) + term, value)

        leaving, starts = lax.scan(advance, begin, correction)
        return (starts, leaving)

    def blank_chain(begin, correction):
        return (jnp.zeros_like(correction), jnp.zeros_like(begin))

    def chain(correction):
        begin = initial_state
        held = jnp.zeros_like(correction)
        for group in range(slices):
            starts, leaving = lax.cond(
                position == group, local_chain, blank_chain, begin, correction
            )
            held = jnp.where(position == group, starts, held)
            if group + 1 < slices:
                arrived = passed_along_2(leaving, "tm", 1)
                begin = jnp.where(position == group + 1, arrived, begin)
        return held

    empty = jnp.zeros((ST_DEV,) + initial_state.shape, jnp.float32)
    start = chain(empty)
    middle = start
    last = start
    for turn in range(ITERS):
        fold = jnp.stack(
            [
                evaluate(start, volume_block, face_blocks),
                evaluate(middle, volume_block, face_blocks),
                evaluate(last, volume_block, face_blocks),
            ]
        )
        first = start + step_length * (
            5.0 / 24.0 * fold[0] + 1.0 / 3.0 * fold[1] - 1.0 / 24.0 * fold[2]
        )
        second = first + 0.5 * step_length * (evaluate(first, volume_block, face_blocks) - fold[1])
        second = second + step_length * (
            -1.0 / 24.0 * fold[0] + 1.0 / 3.0 * fold[1] + 5.0 / 24.0 * fold[2]
        )
        correction = second - coarse(start)
        start = chain(correction)
        middle = first
        last = second
    return (start, last)


def solution(mesh):
    return jax.shard_map(
        per_device,
        mesh=mesh,
        in_specs=(P("space", None, None), P(), P(), P()),
        out_specs=(P("tm", "space", None, None), P("tm", "space", None, None)),
        check_vma=False,
    )
```

profile of v0, /device:TPU:1, one launch (start us, length us, event | category | flops | bytes accessed | tf_op | source)
XLA Modules:
  0.0 147.8 jit_solution(12803668607814460038)
XLA Ops:
  0.7 1.4 conditional.6
  3.4 13.8 %collective-permute-done = f32[1,320,128]{2,1,0:T(8,128)S(1)} collective-permute-done((f32[1,320,128]{2,1,0:T(8,128)}, f32[1,320,128]{2,1,0:T(8,128)S(1)}, u32[]{:S(2)}, u32[]{:S(2)}) %collective-permute-start) | collective-permute-done | bytes 163872 | tf_op jit(solution)/shard_map/ppermute | solution.py:24
  17.3 3.5 %conditional.7 = (f32[2,1,320,128]{3,2,1,0:T(8,128)}) conditional(s32[]{:T(128)} %convert_element_type.4, () %tuple.78, (f32[320,320]{1,0:T(8,128)}, pred[]{:T(512)}, f32[1,320,128]{2,1,0:T(8,128)S(1)}, f32[1,320,128]{2,1,0:T(8,128)}) %tuple.81), branch_computations={%region_4.5_spmd, %region_5.8_spmd} | conditional | flops 157409280 | bytes 3522718 | solution.py:103
  18.3 2.5 %while.67 = (s32[]{:T(128)}, f32[1,320,128]{2,1,0:T(8,128)S(1)}, f32[2,1,320,128]{3,2,1,0:T(8,128)}, f32[320,320]{1,0:T(8,128)S(1)}, s32[]{:T(128)}) while((s32[]{:T(128)}, f32[1,320,128]{2,1,0:T(8,128)S(1)}, f32[2,1,320,128]{3,2,1,0:T(8,128)}, f32[320,320]{1,0:T(8,128)S(1)}, s32[]{:T(128)}) %tuple.207), condition=%wide.region_7.7_spmd, body=%wide.region_6.6_spmd.sunk | while | flops 157368320 | bytes 1392713 | solution.py:93
  23.3 1.9 %collective-permute-start.1 = (f32[2,1,80,128]{3,2,0,1:T(8,128)S(1)}, f32[2,1,80,128]{3,2,0,1:T(8,128)S(1)}, u32[]{:S(2)}, u32[]{:S(2)}) collective-permute-start(f32[2,1,80,128]{3,2,0,1:T(8,128)S(1)} %bitcast.634), channel_id=1, source_target_pairs={{255,0},{0,1},{1,2},{2,3},{3,4},{4,5},{5,6},{6,7},{7,8},{8,9},{9,1... | collective-permute-start | bytes 245768 | tf_op jit(solution)/shard_map/ppermute | solution.py:18
  25.2 10.4 %collective-permute-start.2 = (f32[2,1,80,128]{3,2,0,1:T(8,128)S(1)}, f32[2,1,80,128]{3,2,0,1:T(8,128)S(1)}, u32[]{:S(2)}, u32[]{:S(2)}) collective-permute-start(f32[2,1,80,128]{3,2,0,1:T(8,128)S(1)} %bitcast.630), channel_id=1, source_target_pairs={{1,0},{2,1},{3,2},{4,3},{5,4},{6,5},{7,6},{8,7},{9,8},{10,9},{11,1... | collective-permute-start | bytes 245768 | tf_op jit(solution)/shard_map/ppermute | solution.py:18
  41.1 1.9 %collective-permute-start.3 = (f32[2,1,80,128]{3,2,0,1:T(8,128)S(1)}, f32[2,1,80,128]{3,2,0,1:T(8,128)S(1)}, u32[]{:S(2)}, u32[]{:S(2)}) collective-permute-start(f32[2,1,80,128]{3,2,0,1:T(8,128)S(1)} %bitcast.635), channel_id=1, source_target_pairs={{255,0},{0,1},{1,2},{2,3},{3,4},{4,5},{5,6},{6,7},{7,8},{8,9},{9,1... | collective-permute-start | bytes 245768 | tf_op jit(solution)/shard_map/ppermute | solution.py:18
  43.1 9.1 %collective-permute-start.4 = (f32[2,1,80,128]{3,2,0,1:T(8,128)S(1)}, f32[2,1,80,128]{3,2,0,1:T(8,128)S(1)}, u32[]{:S(2)}, u32[]{:S(2)}) collective-permute-start(f32[2,1,80,128]{3,2,0,1:T(8,128)S(1)} %bitcast.631), channel_id=1, source_target_pairs={{1,0},{2,1},{3,2},{4,3},{5,4},{6,5},{7,6},{8,7},{9,8},{10,9},{11,1... | collective-permute-start | bytes 245768 | tf_op jit(solution)/shard_map/ppermute | solution.py:18
  61.8 1.9 %collective-permute-start.8 = (f32[2,1,80,128]{3,2,0,1:T(8,128)}, f32[2,1,80,128]{3,2,0,1:T(8,128)}, u32[]{:S(2)}, u32[]{:S(2)}) collective-permute-start(f32[2,1,80,128]{3,2,0,1:T(8,128)} %bitcast.132), channel_id=1, source_target_pairs={{255,0},{0,1},{1,2},{2,3},{3,4},{4,5},{5,6},{6,7},{7,8},{8,9},{9,1... | collective-permute-start | bytes 245768 | tf_op jit(solution)/shard_map/ppermute | solution.py:18
  65.8 8.8 %collective-permute-start.9 = (f32[2,1,80,128]{3,2,0,1:T(8,128)S(1)}, f32[2,1,80,128]{3,2,0,1:T(8,128)S(1)}, u32[]{:S(2)}, u32[]{:S(2)}) collective-permute-start(f32[2,1,80,128]{3,2,0,1:T(8,128)S(1)} %bitcast.632), channel_id=1, source_target_pairs={{1,0},{2,1},{3,2},{4,3},{5,4},{6,5},{7,6},{8,7},{9,8},{10,9},{11,1... | collective-permute-start | bytes 245768 | tf_op jit(solution)/shard_map/ppermute | solution.py:18
  77.1 3.5 %conditional.9 = (f32[2,1,320,128]{3,2,1,0:T(8,128)}) conditional(s32[]{:T(128)} %convert_element_type.4, () %tuple.76, (pred[]{:T(512)}, f32[1,320,128]{2,1,0:T(8,128)}, f32[1,320,128]{2,1,0:T(8,128)S(1)}, f32[320,320]{1,0:T(8,128)S(1)}, f32[2,1,320,128]{3,2,0,1:T(8,128)S(1)}) %tuple.213), branch_computations={%region_12.13_spmd, %region_13.16_spmd} | conditional | flops 157450240 | bytes 2293910 | solution.py:103
  78.0 2.5 %while.69 = (s32[]{:T(128)}, f32[1,320,128]{2,1,0:T(8,128)S(1)}, f32[2,1,320,128]{3,2,1,0:T(8,128)}, f32[320,320]{1,0:T(8,128)S(1)}, f32[2,1,320,128]{3,2,1,0:T(8,128)S(1)}, /*index=5*/s32[]{:T(128)}) while((s32[]{:T(128)}, f32[1,320,128]{2,1,0:T(8,128)S(1)}, f32[2,1,320,128]{3,2,1,0:T(8,128)}, f32[320,320]{1,0:T(8,128)S(1)}, ...), condition=%wide.region_15.15_spmd, body=%wide.region_14.14_spmd.sunk | while | flops 157409280 | bytes 1802325 | solution.py:93
  87.3 1.9 %collective-permute-start.6 = (f32[2,1,80,128]{3,2,0,1:T(8,128)S(1)}, f32[2,1,80,128]{3,2,0,1:T(8,128)S(1)}, u32[]{:S(2)}, u32[]{:S(2)}) collective-permute-start(f32[2,1,80,128]{3,2,0,1:T(8,128)S(1)} %bitcast.628), channel_id=1, source_target_pairs={{255,0},{0,1},{1,2},{2,3},{3,4},{4,5},{5,6},{6,7},{7,8},{8,9},{9,1... | collective-permute-start | bytes 245768 | tf_op jit(solution)/shard_map/ppermute | solution.py:18
  89.2 9.1 %collective-permute-start.7 = (f32[2,1,80,128]{3,2,0,1:T(8,128)S(1)}, f32[2,1,80,128]{3,2,0,1:T(8,128)S(1)}, u32[]{:S(2)}, u32[]{:S(2)}) collective-permute-start(f32[2,1,80,128]{3,2,0,1:T(8,128)S(1)} %bitcast.627), channel_id=1, source_target_pairs={{1,0},{2,1},{3,2},{4,3},{5,4},{6,5},{7,6},{8,7},{9,8},{10,9},{11,1... | collective-permute-start | bytes 245768 | tf_op jit(solution)/shard_map/ppermute | solution.py:18
  106.6 1.6 %copy.83 = f32[2,1,80,1,128]{2,0,4,3,1:T(2,128)} copy(f32[2,1,80,1,128]{4,3,2,0,1:T(1,128)} %get-tuple-element.339) | data formatting | bytes 163840
  109.0 1.6 %slice_bitcast_fusion.11 = f32[2,80,121]{1,0,2:T(2,128)} fusion(f32[2,1,80,128]{2,0,3,1:T(2,128)} %bitcast.600), kind=kLoop, calls=%fused_computation.147 | loop fusion | bytes 154880 | tf_op jit(solution)/shard_map/jit(_roll_static)/concatenate | solution.py:48
  111.3 1.6 %copy.84 = f32[2,1,80,1,128]{2,0,4,3,1:T(2,128)} copy(f32[2,1,80,1,128]{4,3,2,0,1:T(1,128)} %get-tuple-element.338) | data formatting | bytes 163840
  114.1 1.9 %collective-permute-start.10 = (f32[2,1,80,128]{3,2,0,1:T(8,128)S(1)}, f32[2,1,80,128]{3,2,0,1:T(8,128)S(1)}, u32[]{:S(2)}, u32[]{:S(2)}) collective-permute-start(f32[2,1,80,128]{3,2,0,1:T(8,128)S(1)} %bitcast.633), channel_id=1, source_target_pairs={{255,0},{0,1},{1,2},{2,3},{3,4},{4,5},{5,6},{6,7},{7,8},{8,9},{9,1... | collective-permute-start | bytes 245768 | tf_op jit(solution)/shard_map/ppermute | solution.py:18
  116.0 9.0 %collective-permute-start.11 = (f32[2,1,80,128]{3,2,0,1:T(8,128)S(1)}, f32[2,1,80,128]{3,2,0,1:T(8,128)S(1)}, u32[]{:S(2)}, u32[]{:S(2)}) collective-permute-start(f32[2,1,80,128]{3,2,0,1:T(8,128)S(1)} %bitcast.629), channel_id=1, source_target_pairs={{1,0},{2,1},{3,2},{4,3},{5,4},{6,5},{7,6},{8,7},{9,8},{10,9},{11,1... | collective-permute-start | bytes 245768 | tf_op jit(solution)/shard_map/ppermute | solution.py:18
  130.4 1.5 conditional.10
  133.2 10.2 %collective-permute-done.12 = f32[1,320,128]{2,1,0:T(8,128)S(1)} collective-permute-done((f32[1,320,128]{2,1,0:T(8,128)}, f32[1,320,128]{2,1,0:T(8,128)S(1)}, u32[]{:S(2)}, u32[]{:S(2)}) %collective-permute-start.12) | collective-permute-done | bytes 163872 | tf_op jit(solution)/shard_map/ppermute | solution.py:24
  143.4 2.6 %conditional.11 = (f32[2,1,320,128]{3,2,1,0:T(8,128)}) conditional(s32[]{:T(128)} %convert_element_type.4, () %tuple.74, (pred[]{:T(512)}, f32[1,320,128]{2,1,0:T(8,128)S(1)}, f32[1,320,128]{2,1,0:T(8,128)S(1)}, f32[320,320]{1,0:T(8,128)S(1)}, f32[2,1,320,128]{3,2,0,1:T(8,128)S(1)}) %tuple.215), branch_computations={%region_20.21_spmd, %region_21.24_spmd} | conditional | flops 157450240 | bytes 2293910 | solution.py:103
  143.4 2.5 %while.71 = (s32[]{:T(128)}, f32[1,320,128]{2,1,0:T(8,128)S(1)}, f32[2,1,320,128]{3,2,1,0:T(8,128)}, f32[320,320]{1,0:T(8,128)S(1)}, f32[2,1,320,128]{3,2,1,0:T(8,128)S(1)}, /*index=5*/s32[]{:T(128)}) while((s32[]{:T(128)}, f32[1,320,128]{2,1,0:T(8,128)S(1)}, f32[2,1,320,128]{3,2,1,0:T(8,128)}, f32[320,320]{1,0:T(8,128)S(1)}, ...), condition=%wide.region_23.23_spmd, body=%wide.region_22.22_spmd.sunk | while | flops 157409280 | bytes 1802325 | solution.py:93
  146.0 1.8 %fusion.56 = f32[2,1,320,128]{3,2,1,0:T(8,128)} fusion(f32[2,1,320,128]{3,2,1,0:T(8,128)} %get-tuple-element.241, f32[2,1,320,128]{3,2,1,0:T(8,128)} %get-tuple-element.684, pred[]{:T(512)S(6)} %eq.73, pred[]{:T(512)} %eq.72), kind=kLoop, calls=%fused_computation.103 | loop fusion | flops 163840 | bytes 983042
  (208 shorter events, 60.4 us)
Async XLA Ops:
  0.6 21.9 %copy-start = (f32[320,320]{1,0:T(8,128)S(1)}, f32[320,320]{1,0:T(8,128)}, u32[]{:S(2)}) copy-start(f32[320,320]{1,0:T(8,128)} %param.29) | copy-start | bytes 1228804
  2.1 15.2 %collective-permute-start = (f32[1,320,128]{2,1,0:T(8,128)}, f32[1,320,128]{2,1,0:T(8,128)S(1)}, u32[]{:S(2)}, u32[]{:S(2)}) collective-permute-start(f32[1,320,128]{2,1,0:T(8,128)} %get-tuple-element.236), channel_id=1, source_target_pairs={{0,256},{1,257},{2,258},{3,259},{4,260},{5,261},{6,262},{7,263},{8... | collective-permute-start | bytes 491528 | tf_op jit(solution)/shard_map/ppermute | solution.py:24
  3.4 49.3 %copy-start.22 = (pred[128]{0:T(512)(128)(4,1)}, pred[128]{0:T(512)(128)(4,1)S(1)}, u32[]{:S(2)}) copy-start(pred[128]{0:T(512)(128)(4,1)S(1)} %broadcast_compare_fusion) | copy-start | bytes 388
  3.4 49.8 %copy-start.20 = (pred[128]{0:T(512)(128)(4,1)}, pred[128]{0:T(512)(128)(4,1)S(1)}, u32[]{:S(2)}) copy-start(pred[128]{0:T(512)(128)(4,1)S(1)} %broadcast_compare_fusion.1) | copy-start | bytes 388
  17.3 1.0 copy-start.3
  22.6 13.1 %copy-start.4 = (f32[6,320,80]{1,2,0:T(8,128)S(1)}, f32[6,320,80]{1,2,0:T(8,128)}, u32[]{:S(2)}) copy-start(f32[6,320,80]{1,2,0:T(8,128)} %param.30) | copy-start | bytes 1843204
  23.3 13.4 %collective-permute-start.1 = (f32[2,1,80,128]{3,2,0,1:T(8,128)S(1)}, f32[2,1,80,128]{3,2,0,1:T(8,128)S(1)}, u32[]{:S(2)}, u32[]{:S(2)}) collective-permute-start(f32[2,1,80,128]{3,2,0,1:T(8,128)S(1)} %bitcast.634), channel_id=1, source_target_pairs={{255,0},{0,1},{1,2},{2,3},{3,4},{4,5},{5,6},{6,7},{7,8},{8,9},{9,1... | collective-permute-start | bytes 245768 | tf_op jit(solution)/shard_map/ppermute | solution.py:18
  25.2 11.9 %collective-permute-start.2 = (f32[2,1,80,128]{3,2,0,1:T(8,128)S(1)}, f32[2,1,80,128]{3,2,0,1:T(8,128)S(1)}, u32[]{:S(2)}, u32[]{:S(2)}) collective-permute-start(f32[2,1,80,128]{3,2,0,1:T(8,128)S(1)} %bitcast.630), channel_id=1, source_target_pairs={{1,0},{2,1},{3,2},{4,3},{5,4},{6,5},{7,6},{8,7},{9,8},{10,9},{11,1... | collective-permute-start | bytes 245768 | tf_op jit(solution)/shard_map/ppermute | solution.py:18
  41.1 12.4 %collective-permute-start.3 = (f32[2,1,80,128]{3,2,0,1:T(8,128)S(1)}, f32[2,1,80,128]{3,2,0,1:T(8,128)S(1)}, u32[]{:S(2)}, u32[]{:S(2)}) collective-permute-start(f32[2,1,80,128]{3,2,0,1:T(8,128)S(1)} %bitcast.635), channel_id=1, source_target_pairs={{255,0},{0,1},{1,2},{2,3},{3,4},{4,5},{5,6},{6,7},{7,8},{8,9},{9,1... | collective-permute-start | bytes 245768 | tf_op jit(solution)/shard_map/ppermute | solution.py:18
  43.1 11.0 %collective-permute-start.4 = (f32[2,1,80,128]{3,2,0,1:T(8,128)S(1)}, f32[2,1,80,128]{3,2,0,1:T(8,128)S(1)}, u32[]{:S(2)}, u32[]{:S(2)}) collective-permute-start(f32[2,1,80,128]{3,2,0,1:T(8,128)S(1)} %bitcast.631), channel_id=1, source_target_pairs={{1,0},{2,1},{3,2},{4,3},{5,4},{6,5},{7,6},{8,7},{9,8},{10,9},{11,1... | collective-permute-start | bytes 245768 | tf_op jit(solution)/shard_map/ppermute | solution.py:18
  55.5 1.0 copy-start.1
  59.6 17.4 %collective-permute-start.5 = (f32[1,320,128]{2,1,0:T(8,128)}, f32[1,320,128]{2,1,0:T(8,128)}, u32[]{:S(2)}, u32[]{:S(2)}) collective-permute-start(f32[1,320,128]{2,1,0:T(8,128)} %get-tuple-element.238), channel_id=1, source_target_pairs={{0,256},{1,257},{2,258},{3,259},{4,260},{5,261},{6,262},{7,263},{8... | collective-permute-start | bytes 491528 | tf_op jit(solution)/shard_map/ppermute | solution.py:24
  61.8 12.8 %collective-permute-start.8 = (f32[2,1,80,128]{3,2,0,1:T(8,128)}, f32[2,1,80,128]{3,2,0,1:T(8,128)}, u32[]{:S(2)}, u32[]{:S(2)}) collective-permute-start(f32[2,1,80,128]{3,2,0,1:T(8,128)} %bitcast.132), channel_id=1, source_target_pairs={{255,0},{0,1},{1,2},{2,3},{3,4},{4,5},{5,6},{6,7},{7,8},{8,9},{9,1... | collective-permute-start | bytes 245768 | tf_op jit(solution)/shard_map/ppermute | solution.py:18
  65.8 10.3 %collective-permute-start.9 = (f32[2,1,80,128]{3,2,0,1:T(8,128)S(1)}, f32[2,1,80,128]{3,2,0,1:T(8,128)S(1)}, u32[]{:S(2)}, u32[]{:S(2)}) collective-permute-start(f32[2,1,80,128]{3,2,0,1:T(8,128)S(1)} %bitcast.632), channel_id=1, source_target_pairs={{1,0},{2,1},{3,2},{4,3},{5,4},{6,5},{7,6},{8,7},{9,8},{10,9},{11,1... | collective-permute-start | bytes 245768 | tf_op jit(solution)/shard_map/ppermute | solution.py:18
  83.2 1.1 copy-start.9
  85.7 1.4 copy-start.8
  87.3 14.1 %collective-permute-start.6 = (f32[2,1,80,128]{3,2,0,1:T(8,128)S(1)}, f32[2,1,80,128]{3,2,0,1:T(8,128)S(1)}, u32[]{:S(2)}, u32[]{:S(2)}) collective-permute-start(f32[2,1,80,128]{3,2,0,1:T(8,128)S(1)} %bitcast.628), channel_id=1, source_target_pairs={{255,0},{0,1},{1,2},{2,3},{3,4},{4,5},{5,6},{6,7},{7,8},{8,9},{9,1... | collective-permute-start | bytes 245768 | tf_op jit(solution)/shard_map/ppermute | solution.py:18
  89.2 12.7 %collective-permute-start.7 = (f32[2,1,80,128]{3,2,0,1:T(8,128)S(1)}, f32[2,1,80,128]{3,2,0,1:T(8,128)S(1)}, u32[]{:S(2)}, u32[]{:S(2)}) collective-permute-start(f32[2,1,80,128]{3,2,0,1:T(8,128)S(1)} %bitcast.627), channel_id=1, source_target_pairs={{1,0},{2,1},{3,2},{4,3},{5,4},{6,5},{7,6},{8,7},{9,8},{10,9},{11,1... | collective-permute-start | bytes 245768 | tf_op jit(solution)/shard_map/ppermute | solution.py:18
  98.4 1.1 copy-start.19
  98.4 1.1 copy-start.25
  108.3 2.3 %copy-start.11 = (f32[2,1,80,1,128]{2,0,4,3,1:T(2,128)S(1)}, f32[2,1,80,1,128]{2,0,4,3,1:T(2,128)}, u32[]{:S(2)}) copy-start(f32[2,1,80,1,128]{2,0,4,3,1:T(2,128)} %copy.83) | copy-start | bytes 245764
  114.1 12.4 %collective-permute-start.10 = (f32[2,1,80,128]{3,2,0,1:T(8,128)S(1)}, f32[2,1,80,128]{3,2,0,1:T(8,128)S(1)}, u32[]{:S(2)}, u32[]{:S(2)}) collective-permute-start(f32[2,1,80,128]{3,2,0,1:T(8,128)S(1)} %bitcast.633), channel_id=1, source_target_pairs={{255,0},{0,1},{1,2},{2,3},{3,4},{4,5},{5,6},{6,7},{7,8},{8,9},{9,1... | collective-permute-start | bytes 245768 | tf_op jit(solution)/shard_map/ppermute | solution.py:18
  116.0 11.7 %collective-permute-start.11 = (f32[2,1,80,128]{3,2,0,1:T(8,128)S(1)}, f32[2,1,80,128]{3,2,0,1:T(8,128)S(1)}, u32[]{:S(2)}, u32[]{:S(2)}) collective-permute-start(f32[2,1,80,128]{3,2,0,1:T(8,128)S(1)} %bitcast.629), channel_id=1, source_target_pairs={{1,0},{2,1},{3,2},{4,3},{5,4},{6,5},{7,6},{8,7},{9,8},{10,9},{11,1... | collective-permute-start | bytes 245768 | tf_op jit(solution)/shard_map/ppermute | solution.py:18
  131.9 11.5 %collective-permute-start.12 = (f32[1,320,128]{2,1,0:T(8,128)}, f32[1,320,128]{2,1,0:T(8,128)S(1)}, u32[]{:S(2)}, u32[]{:S(2)}) collective-permute-start(f32[1,320,128]{2,1,0:T(8,128)} %get-tuple-element.240), channel_id=1, source_target_pairs={{0,256},{1,257},{2,258},{3,259},{4,260},{5,261},{6,262},{7,263},{8... | collective-permute-start | bytes 491528 | tf_op jit(solution)/shard_map/ppermute | solution.py:24
  (14 other events, 12.0 us)
where the time goes:
time: 149 us; the launch traced here: 148 us
  starting transfers between devices  59.8 us (40%)
  local copies, waits for them, and re-layouts  30.4 us (20%)
  matrix products  24.5 us (16%)
  waiting for transfers between devices  24.1 us (16%)
  other arithmetic  6.88 us (5%)
  between operations  1.83 us (1%)
    ppermute x10, starting transfers between devices, passed_along(): return lax.ppermute(block, axis, route)  56 us
    dot_general x43, matrix products, apply(): jnp.einsum('ab,...bq->...aq', block, field, precision=lax.Precision.HIGHEST)  24.5 us
    ppermute x3, waiting for transfers between devices, passed_along_2(): return lax.ppermute(shard, axis, pairs)  24.1 us
    unnamed x58, local copies, waits for them, and re-layouts  9.85 us
    another operation x6, local copies, waits for them, and re-layouts  4.29 us
    dynamic_update_slice x6, local copies, waits for them, and re-layouts, local_chain(): leaving, starts = lax.scan(advance, begin, correction)  4.1 us
    ppermute x3, starting transfers between devices, passed_along_2(): return lax.ppermute(shard, axis, pairs)  3.84 us
    concatenate x8, local copies, waits for them, and re-layouts, along_z(): wrapped = jnp.roll(trace, -(EZ - 1), axis=-1)  3.71 us
  transfers between devices with their start and end apart: 13, of which 2 were waited for; matrix products, arithmetic and copies ran while one was open for 8% of the time, Pallas kernels for 0%

commit v1 on v0

v1 whole, which is shorter than its diff:
```python
import functools

import jax
import jax.numpy as jnp
from jax import lax
from jax.experimental import pallas as pl
from jax.experimental.pallas import tpu as pltpu
from jax.sharding import PartitionSpec as P

F = 5
EZ = 8
FP = 320
FACE = 80
EYZ = 128
NT = 4
ROW = 4
HALO = 4
WIN = 2 * HALO + 1
KR = FP + 6 * FACE
BF = jnp.bfloat16
F32 = jnp.float32


def split(value):
    high = value.astype(BF)
    low = (value - high.astype(F32)).astype(BF)
    return high, low


def x_rows(piece, level):
    return jnp.concatenate(
        [piece[f * 64 + 16 * level : f * 64 + 16 * level + 16] for f in range(F)], axis=0
    )


def y_face(value, level):
    wide = value.reshape(10, 32, EYZ)
    half = 8 * (level // 2)
    first, second = wide[:, half : half + 8], wide[:, 16 + half : 24 + half]
    upper_half = lax.broadcasted_iota(jnp.int32, (10, 8, EYZ), 1) >= 4
    if level % 2 == 1:
        first = pltpu.roll(first, 4, 1)
    else:
        second = pltpu.roll(second, 4, 1)
    return jnp.where(upper_half, second, first).reshape(FACE, EYZ)


def kernel(
    where,
    own,
    far,
    near,
    op_r,
    op_c,
    starts,
    ends,
    y,
    u1,
    u2,
    yp,
    w,
    v1,
    b,
    bc,
    up_op,
    lo_op,
):
    core, col, odd_row = where[0], where[1], where[2]

    y[HALO, 0] = own[...]
    y[2 * HALO, 0] = far[odd_row]
    y[0, 0] = far[1 - odd_row]

    def place(mate, own_block, other_block):
        y[mate - col + HALO, 0] = own_block
        y[jnp.where(mate > col, mate - col, mate - col + WIN - 1), 0] = other_block

    place(col + 1 - 2 * lax.rem(col, 2), near[0, 0:FP], near[0, FP : 2 * FP])
    place(ROW - 1 - col, near[1, 0:FP], near[1, FP : 2 * FP])
    place(lax.rem(col + 2, ROW), near[0, 2 * FP : 3 * FP], near[1, 2 * FP : 3 * FP])

    for f in range(F):
        up_op[16 * f : 16 * f + 16] = op_r[64 * f + 48 : 64 * f + 64]
        lo_op[16 * f : 16 * f + 16] = op_r[64 * f : 64 * f + 16]

    lane = lax.broadcasted_iota(jnp.int32, (FACE, EYZ), 1) % EZ

    def put(base, rows, lanes, value, size):
        high, low = split(value)
        b[base : base + rows, lanes] = high
        b[KR + base : KR + base + rows, lanes] = high
        b[2 * KR + base : 2 * KR + base + rows, lanes] = low

    def gather(state, at, minus_x, plus_x):
        for s in range(NT):
            lanes = slice(EYZ * s, EYZ * (s + 1))
            value = state[at, s]
            put(0, FP, lanes, value, FP)
            put(FP, FACE, lanes, minus_x(s), FACE)
            put(FP + FACE, FACE, lanes, plus_x(s), FACE)
            put(FP + 2 * FACE, FACE, lanes, pltpu.roll(y_face(value, 3), EZ, 1), FACE)
            put(FP + 3 * FACE, FACE, lanes, pltpu.roll(y_face(value, 0), EYZ - EZ, 1), FACE)
            low_z = state[at, s, pl.ds(3, FACE, stride=4), :]
            high_z = state[at, s, pl.ds(0, FACE, stride=4), :]
            put(
                FP + 4 * FACE,
                FACE,
                lanes,
                jnp.where(lane == 0, pltpu.roll(low_z, EYZ - EZ + 1, 1), pltpu.roll(low_z, 1, 1)),
                FACE,
            )
            put(
                FP + 5 * FACE,
                FACE,
                lanes,
                jnp.where(
                    lane == EZ - 1, pltpu.roll(high_z, EZ - 1, 1), pltpu.roll(high_z, EYZ - 1, 1)
                ),
                FACE,
            )

    def x_face(state, at, level):
        return lambda s: x_rows(state[at, s], level)

    def dot(left, right):
        return jnp.dot(left, right, preferred_element_type=F32)

    def lanes_of(product, s):
        return product[:, EYZ * s : EYZ * (s + 1)]

    def coarse(values):
        for k, value in enumerate(values):
            lanes = slice(EYZ * k, EYZ * (k + 1))
            high, low = split(value)
            bc[0:FP, lanes] = high
            bc[FP : 2 * FP, lanes] = high
            bc[2 * FP : 3 * FP, lanes] = low
        product = dot(op_c[...], bc[:, : EYZ * len(values)])
        return [value + lanes_of(product, k) for k, value in enumerate(values)]

    for n in range(NT - 1):
        for k, value in enumerate(coarse([y[k, n] for k in range(WIN)])):
            y[k, n + 1] = value

    def first_node(k, carry):
        gather(y, k + 1, x_face(y, k, 3), x_face(y, k + 2, 0))
        product = dot(op_r[...], b[...])
        for s in range(NT):
            u1[k, s] = y[k + 1, s] + lanes_of(product, s)
        return carry

    lax.fori_loop(0, 7, first_node, 0)

    def second_node(k, carry):
        gather(u1, k + 1, x_face(u1, k, 3), x_face(u1, k + 2, 0))
        product = dot(op_r[...], b[...])
        for s in range(NT):
            u2[k, s] = u1[k + 1, s] + lanes_of(product, s)
        return carry

    lax.fori_loop(0, 5, second_node, 0)

    for k in range(5):
        yp[k, 0] = y[k + 2, 0]
        yp[k, 1] = u2[k, 0]
    for n in (1, 2):
        change = coarse([yp[k, n] - y[k + 2, n] for k in range(5)])
        for k in range(5):
            yp[k, n + 1] = u2[k, n] + change[k]

    for k in range(5):
        for s in range(NT):
            w[k, s] = (5.0 / 12.0) * yp[k, s] + (2.0 / 3.0) * u1[k + 1, s] - (1.0 / 12.0) * u2[k, s]

    gather(w, 2, x_face(w, 1, 3), x_face(w, 3, 0))
    product = dot(op_r[...], b[...])
    for s in range(NT):
        v1[s] = (1.0 / 3.0) * (yp[2, s] + u1[3, s] + u2[2, s]) + (
            yp[2, s] + lanes_of(product, s)
        )

    sides = []
    for at, level, op in ((1, 3, up_op), (3, 0, lo_op)):
        gather(w, at, x_face(w, at - 1, 3), x_face(w, at + 1, 0))
        product = dot(op[...], b[...])
        side = []
        for s in range(NT):
            start = x_rows(yp[at, s], level)
            side.append(
                (1.0 / 3.0) * (start + x_rows(u1[at + 1, s], level) + x_rows(u2[at, s], level))
                + (start + lanes_of(product, s))
            )
        sides.append(side)
    for s in range(NT):
        w[2, s] = v1[s]
    gather(w, 2, lambda s: sides[0][s], lambda s: sides[1][s])
    product = dot(op_r[...], b[...])
    last = [yp[2, s] + lanes_of(product, s) for s in range(NT)]

    begin = [own[...], last[0]]
    for n in (1, 2):
        begin.append(last[n] + coarse([begin[n] - yp[2, n]])[0])

    @pl.when(core == 0)
    def _():
        for k in range(2):
            starts[k] = begin[k]
            ends[k] = last[k]

    @pl.when(core == 1)
    def _():
        for k in range(2):
            starts[k] = begin[2 + k]
            ends[k] = last[2 + k]


def work(where, own, far, near, op_r, op_c):
    vmem = pl.BlockSpec(memory_space=pltpu.VMEM)
    out = jax.ShapeDtypeStruct((2, FP, EYZ), F32)
    return pl.pallas_call(
        kernel,
        out_shape=(out, out),
        in_specs=[pl.BlockSpec(memory_space=pltpu.SMEM)] + [vmem] * 5,
        out_specs=(vmem, vmem),
        scratch_shapes=[
            pltpu.VMEM((WIN, NT, FP, EYZ), F32),
            pltpu.VMEM((7, NT, FP, EYZ), F32),
            pltpu.VMEM((5, NT, FP, EYZ), F32),
            pltpu.VMEM((5, NT, FP, EYZ), F32),
            pltpu.VMEM((5, NT, FP, EYZ), F32),
            pltpu.VMEM((NT, FP, EYZ), F32),
            pltpu.VMEM((3 * KR, NT * EYZ), BF),
            pltpu.VMEM((3 * FP, WIN * EYZ), BF),
            pltpu.VMEM((FACE, 3 * KR), BF),
            pltpu.VMEM((FACE, 3 * KR), BF),
        ],
        compiler_params=pltpu.CompilerParams(vmem_limit_bytes=48 << 20),
        name="parareal",
    )(where, own, far, near, op_r, op_c)


def operator(block):
    high = lax.reduce_precision(block, 8, 7)
    low = block - high
    return jnp.concatenate([high, low, high], axis=1).astype(BF)


def pairs(mate_of, spaces):
    groups = []
    for core in range(2):
        for place in range(spaces):
            mate = mate_of(core, place)
            assert mate_of(core, mate) == place
            if place < mate:
                groups.append([core * spaces + place, core * spaces + mate])
    return groups


def swapped(block, mate_of, spaces):
    both = lax.all_gather(block, ("tm", "space"), axis_index_groups=pairs(mate_of, spaces))
    core, place = lax.axis_index("tm"), lax.axis_index("space")
    mate = mate_of(core, place)
    return jnp.where(mate > place, both[1], both[0])


def other_row(spaces):
    def mate_of(core, place):
        down = (place // ROW + core) % 2
        return (place + ROW - 2 * ROW * down + spaces) % spaces

    return mate_of


def row_near(core, place):
    base, col = place // ROW * ROW, place % ROW
    return base + (1 - core) * (col + 1 - 2 * (col % 2)) + core * (ROW - 1 - col)


def row_far(core, place):
    return place // ROW * ROW + (place % ROW + 2) % ROW


def per_device(initial_state, volume_block, face_blocks, coarse_rate):
    spaces = lax.axis_size("space")
    core, place = lax.axis_index("tm"), lax.axis_index("space")
    col, odd_row = place % ROW, place // ROW % 2
    own = initial_state[0]

    across = swapped(own, other_row(spaces), spaces)
    far = lax.all_gather(across, "tm")
    above, below = far[odd_row], far[1 - odd_row]

    gives_above = jnp.where(core == 0, col % 2 == 0, col < 2)
    close = swapped(
        jnp.concatenate([own, jnp.where(gives_above, above, below)], axis=0), row_near, spaces
    )
    distant = swapped(
        jnp.where(core == 0, own, jnp.where(col < 2, above, below)), row_far, spaces
    )
    near = lax.all_gather(jnp.concatenate([close, distant], axis=0), "tm")

    step = 0.25
    blocks = jnp.concatenate([volume_block] + [face_blocks[k] for k in range(6)], axis=1)
    op_r = operator(0.5 * step * blocks)
    op_c = operator(step * coarse_rate)
    where = jnp.stack([core, col, odd_row]).astype(jnp.int32)
    starts, ends = work(where, own, far, near, op_r, op_c)
    return starts[:, None], ends[:, None]


def solution(mesh):
    return jax.shard_map(
        per_device,
        mesh=mesh,
        in_specs=(P("space", None, None), P(), P(), P()),
        out_specs=(P("tm", "space", None, None), P("tm", "space", None, None)),
        check_vma=False,
    )
```

time: 149 us -> 73.4 us (0.49)
  starting transfers between devices: 59.8 us -> 0 us
  blocking collectives: 0 us -> 37.2 us
  Pallas kernels: 0 us -> 27.7 us
  local copies, waits for them, and re-layouts: 30.4 us -> 5.78 us
  matrix products: 24.5 us -> 0 us
  waiting for transfers between devices: 24.1 us -> 0 us
  other arithmetic: 6.88 us -> 1.69 us
    ppermute x13 -> x0, starting transfers between devices: 59.8 us -> none  [the longest x10 56 us: passed_along(): return lax.ppermute(block, axis, route)]
    all_gather x0 -> x5, blocking collectives: none -> 37.2 us  [the longest x3 32 us: swapped(): lax.all_gather(block, ('tm', 'space'), axis_index_groups=pairs(mate_of, s...]
    pallas_call x0 -> x1, Pallas kernels: none -> 27.7 us  [work(): pl.pallas_call(kernel, out_shape=(out, out), in_specs=[pl.BlockSpec(memor...]
    dot_general x43 -> x0, matrix products: 24.5 us -> none  [apply(): jnp.einsum('ab,...bq->...aq', block, field, precision=lax.Precision.HIGHEST)]
    ppermute x13 -> x0, waiting for transfers between devices: 24.1 us -> none  [the longest x3 24.1 us: passed_along_2(): return lax.ppermute(shard, axis, pairs)]
    unnamed x58 -> x12, local copies, waits for them, and re-layouts: 9.85 us -> 1.35 us
    select_n x13 -> x4, other arithmetic: 5.02 us -> 0.1 us  [the longest x3 0.07 us: swapped(): return jnp.where(mate > place, both[1], both[0])]
    another operation x6 -> x0, local copies, waits for them, and re-layouts: 4.29 us -> none
  transfers between devices with their start and end apart: 13 -> 0, of which waited for: 2 -> 0; matrix products, arithmetic and copies ran while one was open for 8% -> 0% of each run, Pallas kernels for 0% -> 0%
where the time goes in v1:
time: 73.4 us; the launch traced here: 73.2 us
  blocking collectives  37.2 us (51%)
  Pallas kernels  27.7 us (38%)
  local copies, waits for them, and re-layouts  5.78 us (8%)
  other arithmetic  1.69 us (2%)
  between operations  0.81 us (1%)
    all_gather x3, blocking collectives, swapped(): lax.all_gather(block, ('tm', 'space'), axis_index_groups=pairs(mate_of, s...  32 us
    pallas_call x1, Pallas kernels, work(): pl.pallas_call(kernel, out_shape=(out, out), in_specs=[pl.BlockSpec(memor...  27.7 us
    all_gather x1, blocking collectives, per_device(): near = lax.all_gather(jnp.concatenate([close, distant], axis=0), 'tm')  3.13 us
    concatenate x1, local copies, waits for them, and re-layouts, operator(): return jnp.concatenate([high, low, high], axis=1).astype(BF)  2.9 us
    all_gather x1, blocking collectives, per_device(): far = lax.all_gather(across, 'tm')  2.04 us
    concatenate x1, local copies, waits for them, and re-layouts, per_device(): jnp.concatenate([volume_block] + [face_blocks[k] for k in range(6)], axis=1)  1.48 us

profile of v1, /device:TPU:1, one launch (start us, length us, event | category | flops | bytes accessed | tf_op | source)
XLA Modules:
  0.0 73.2 jit_solution(5814464093105534568)
XLA Ops:
  0.6 0.0 copy-start
  0.7 16.3 %all_gather.23 = f32[2,320,128]{2,1,0:T(8,128)S(1)} all-gather(f32[1,320,128]{2,1,0:T(8,128)} %param.4), channel_id=1, replica_groups={{0,4},{1,5},{2,6},{3,7},{8,12},{9,13},{10,14},{11,15},{16,20},{17,21},{..., dimensions={0}, use_global_device_ids=true | all-gather | bytes 491520 | tf_op jit(solution)/shard_map/all_gather | solution.py:260
  17.0 2.0 %all_gather.24.far = f32[2,320,128]{2,1,0:T(8,128)S(1)} all-gather(f32[1,320,128]{2,1,0:T(8,128)S(1)} %slice_select_fusion.2), channel_id=1, replica_groups=mesh['tm'=2,'space'=256] {'tm'}, dimensions={0}, use_global_device_ids=true | all-gather | bytes 491520 | tf_op jit(solution)/shard_map/all_gather | solution.py:290
  19.0 0.0 copy-done
  19.1 7.8 %all-gather = f32[1280,128]{1,0:T(8,128)S(1)} all-gather(f32[640,128]{1,0:T(8,128)S(1)} %pad_maximum_fusion.2), channel_id=2, replica_groups={{0,1},{2,3},{4,5},{6,7},{8,9},{10,11},{12,13},{14,15},{16,17},{18,19},{..., dimensions={0}, use_global_device_ids=true | all-gather | bytes 983040 | tf_op jit(solution)/shard_map/all_gather | solution.py:260
  26.9 7.9 %all_gather.27 = f32[2,320,128]{2,1,0:T(8,128)S(1)} all-gather(f32[1,320,128]{2,1,0:T(8,128)S(1)} %get-tuple-element.21), channel_id=1, replica_groups={{0,2},{1,3},{4,6},{5,7},{8,10},{9,11},{12,14},{13,15},{16,18},{17,19},{..., dimensions={0}, use_global_device_ids=true | all-gather | bytes 491520 | tf_op jit(solution)/shard_map/all_gather | solution.py:260
  34.9 0.0 copy-start.1
  35.0 3.1 %all-gather.1 = f32[1920,128]{1,0:T(8,128)S(1)} all-gather(f32[960,128]{1,0:T(8,128)S(1)} %pad_maximum_fusion.1), channel_id=3, replica_groups=mesh['tm'=2,'space'=256] {'tm'}, dimensions={0}, use_global_device_ids=true | all-gather | bytes 1474560 | tf_op jit(solution)/shard_map/all_gather | solution.py:300
  38.1 0.1 pad_add_fusion.where
  38.2 0.0 copy-done.1
  38.2 0.1 copy.25
  38.3 0.1 copy.26
  38.4 0.1 copy.27
  38.6 0.1 copy.22
  38.7 0.1 copy.23
  38.8 0.8 %copy.24 = f32[1,320,80]{2,1,0:T(8,128)} copy(f32[1,320,80]{1,2,0:T(8,128)S(1)} %get-tuple-element.15) | data formatting | bytes 204800
  39.6 1.5 %concatenate.19 = f32[320,800]{1,0:T(8,128)S(1)} concatenate(f32[320,320]{1,0:T(8,128)} %param.5, f32[320,80]{1,0:T(8,128)S(1)} %bitcast.27, f32[320,80]{1,0:T(8,128)S(1)} %bitcast.28, f32[320,80]{1,0:T(8,128)} %bitcast.29, f32[320,80]{1,0:T(8,128)S(1)} %bitcast.24, f32[320,80]{1,0:T(8,128)S(1)} %bitcast.25, f32[320,80]{1,0:T(8,128)S(1)} %bitcast.26), dimensions={1} | concatenate | bytes 2048000 | tf_op jit(solution)/shard_map/concatenate | solution.py:303
  41.1 1.2 %fusion = (bf16[320,800]{1,0:T(8,128)(2,1)}, bf16[320,800]{1,0:T(8,128)(2,1)}) fusion(f32[320,800]{1,0:T(8,128)S(1)} %concatenate.19), kind=kLoop, calls=%fused_computation.2 | loop fusion | flops 1280000 | bytes 2048000 | tf_op jit(solution)/shard_map/convert.4
  42.3 0.0 copy-start.2
  42.3 2.9 %concatenate.20.op_r = bf16[320,2400]{1,0:T(8,128)(2,1)S(1)} concatenate(bf16[320,800]{1,0:T(8,128)(2,1)} %get-tuple-element.11, bf16[320,800]{1,0:T(8,128)(2,1)} %get-tuple-element.10, bf16[320,800]{1,0:T(8,128)(2,1)} %get-tuple-element.11), dimensions={1} | concatenate | bytes 3072000 | tf_op jit(solution)/shard_map/concatenate | solution.py:245
  45.2 0.0 copy-done.2
  45.2 0.1 fusion.1
  45.3 0.2 pad_maximum_fusion.op_c
  45.5 27.7 %parareal.1 = (f32[2,320,128]{2,1,0:T(8,128)}, f32[2,320,128]{2,1,0:T(8,128)}) custom-call(s32[3]{0:T(128)S(1)} %pad_add_fusion.where, f32[320,128]{1,0:T(8,128)S(1)} %bitcast.23, f32[2,320,128]{2,1,0:T(8,128)S(1)} %all_gather.24.far, f32[2,960,128]{2,1,0:T(8,128)S(1)} %bitcast.21, bf16[320,2400]{1,0:T(8,128)(2,1)S(1)} %concatenate.20.op_r, ...), custom_call_target="tpu_custom_call" | custom-call | tf_op jit(solution)/shard_map/parareal/pallas_call | solution.py:220
  (7 shorter events, 0.2 us)
Async XLA Ops:
  0.6 18.4 %copy-start = (f32[1,320,128]{2,1,0:T(8,128)S(1)}, f32[1,320,128]{2,1,0:T(8,128)}, u32[]{:S(2)}) copy-start(f32[1,320,128]{2,1,0:T(8,128)} %param.4) | copy-start | bytes 491524
  34.9 3.3 %copy-start.1 = (f32[6,320,80]{1,2,0:T(8,128)S(1)}, f32[6,320,80]{1,2,0:T(8,128)}, u32[]{:S(2)}) copy-start(f32[6,320,80]{1,2,0:T(8,128)} %param.6) | copy-start | bytes 1843204
  42.3 2.9 %copy-start.2 = (f32[320,320]{1,0:T(8,128)S(1)}, f32[320,320]{1,0:T(8,128)}, u32[]{:S(2)}) copy-start(f32[320,320]{1,0:T(8,128)} %param.7) | copy-start | bytes 1228804

commit v2 on v1

v2 whole, which is shorter than its diff:
```python
import functools

import jax
import jax.numpy as jnp
from jax import lax
from jax.experimental import pallas as pl
from jax.experimental.pallas import tpu as pltpu
from jax.sharding import PartitionSpec as P

F = 5
EZ = 8
FP = 320
FACE = 80
EYZ = 128
NT = 4
ROW = 4
HALO = 4
WIN = 2 * HALO + 1
KR = FP + 6 * FACE
MAIN = 768
REST = KR - MAIN
CMAIN = 256
CREST = FP - CMAIN
BF = jnp.bfloat16
F32 = jnp.float32


def split(value):
    high = value.astype(BF)
    low = (value - high.astype(F32)).astype(BF)
    return high, low


def dot(left, right):
    return jnp.dot(left, right, preferred_element_type=F32)


def dot_first(left, right):
    return lax.dot_general(left, right, (((0,), (0,)), ((), ())), preferred_element_type=F32)


def x_rows(piece, level):
    return jnp.concatenate(
        [piece[f * 64 + 16 * level : f * 64 + 16 * level + 16] for f in range(F)], axis=0
    )


def y_face(value, level):
    wide = value.reshape(10, 32, EYZ)
    half = 8 * (level // 2)
    first, second = wide[:, half : half + 8], wide[:, 16 + half : 24 + half]
    upper_half = lax.broadcasted_iota(jnp.int32, (10, 8, EYZ), 1) >= 4
    if level % 2 == 1:
        first = pltpu.roll(first, 4, 1)
    else:
        second = pltpu.roll(second, 4, 1)
    return jnp.where(upper_half, second, first).reshape(FACE, EYZ)


def lanes_of(product, s):
    return product[:, EYZ * s : EYZ * (s + 1)]


def side_by_side(ref, high, low, main, rest):
    for k, part in enumerate((high, low, high)):
        ref[:, main * k : main * (k + 1)] = part[:, :main]
        ref[:, 3 * main + rest * k : 3 * main + rest * (k + 1)] = part[:, main:]


def coarse(op_c, bc, values):
    for k, value in enumerate(values):
        lanes = slice(EYZ * k, EYZ * (k + 1))
        high, low = split(value)
        for j, part in enumerate((high, high, low)):
            bc[CMAIN * j : CMAIN * (j + 1), lanes] = part[:CMAIN]
            bc[3 * CMAIN + CREST * j : 3 * CMAIN + CREST * (j + 1), lanes] = part[CMAIN:]
    product = dot(op_c[...], bc[:, : EYZ * len(values)])
    return [value + lanes_of(product, k) for k, value in enumerate(values)]


def prepare(own, far, volume, faces, rate, op_r, op_c, y, bc):
    step = 0.25
    side_by_side(op_c, *split(step * rate[...]), CMAIN, CREST)
    for k, start in enumerate((own[...], far[0], far[1])):
        y[k, 0] = start
    for n in range(NT - 1):
        for k, value in enumerate(coarse(op_c, bc, [y[k, n] for k in range(3)])):
            y[k, n + 1] = value

    def placed(rows, first):
        at = lax.broadcasted_iota(jnp.int32, (rows, KR), 0) + first
        return jnp.where(at == lax.broadcasted_iota(jnp.int32, (rows, KR), 1), 1.0, 0.0).astype(BF)

    here, there = placed(FP, 0), placed(6 * FACE, FP)
    volumes = split(0.5 * step * volume[...])
    fluxes = split(0.5 * step * faces[...])
    high, low = [
        (dot(v, here) + dot_first(f, there)).astype(BF) for v, f in zip(volumes, fluxes)
    ]
    side_by_side(op_r, high, low, MAIN, REST)


def sweeps(where, ready, near, op_r, op_c, starts, ends, y, u1, u2, yp, w, b0, b1, bc, up_op, lo_op):
    core, col, odd_row = where[0], where[1], where[2]

    def place(mate, own_block, other_block):
        y[mate - col + HALO, 0] = own_block
        y[jnp.where(mate > col, mate - col, mate - col + WIN - 1), 0] = other_block

    place(col + 1 - 2 * lax.rem(col, 2), near[0, 0:FP], near[0, FP : 2 * FP])
    place(ROW - 1 - col, near[1, 0:FP], near[1, FP : 2 * FP])
    place(lax.rem(col + 2, ROW), near[0, 2 * FP : 3 * FP], near[1, 2 * FP : 3 * FP])
    for s in range(NT):
        y[HALO, s] = ready[0, s]
        y[2 * HALO, s] = ready[1 + odd_row, s]
        y[0, s] = ready[2 - odd_row, s]

    for f in range(F):
        up_op[16 * f : 16 * f + 16] = op_r[64 * f + 48 : 64 * f + 64]
        lo_op[16 * f : 16 * f + 16] = op_r[64 * f : 64 * f + 16]

    lane = lax.broadcasted_iota(jnp.int32, (FACE, EYZ), 1) % EZ

    def put(b, base, lanes, value):
        rows = value.shape[0]
        whole = min(rows, MAIN - base)
        high, low = split(value)
        for k, part in enumerate((high, high, low)):
            b[MAIN * k + base : MAIN * k + base + whole, lanes] = part[:whole]
            if whole < rows:
                b[3 * MAIN + REST * k : 3 * MAIN + REST * (k + 1), lanes] = part[whole:]

    def gather(b, state, at, minus_x, plus_x, slices=range(NT)):
        for s in slices:
            lanes = slice(EYZ * s, EYZ * (s + 1))
            value = state[at, s]
            put(b, 0, lanes, value)
            put(b, FP, lanes, minus_x(s))
            put(b, FP + FACE, lanes, plus_x(s))
            put(b, FP + 2 * FACE, lanes, pltpu.roll(y_face(value, 3), EZ, 1))
            put(b, FP + 3 * FACE, lanes, pltpu.roll(y_face(value, 0), EYZ - EZ, 1))
            low_z = state[at, s, pl.ds(3, FACE, stride=4), :]
            high_z = state[at, s, pl.ds(0, FACE, stride=4), :]
            low_z = jnp.where(
                lane == 0, pltpu.roll(low_z, EYZ - EZ + 1, 1), pltpu.roll(low_z, 1, 1)
            )
            high_z = jnp.where(
                lane == EZ - 1, pltpu.roll(high_z, EZ - 1, 1), pltpu.roll(high_z, EYZ - 1, 1)
            )
            put(b, FP + 4 * FACE, lanes, low_z)
            put(b, FP + 5 * FACE, lanes, high_z)

    def x_face(state, at, level):
        return lambda s: x_rows(state[at, s], level)

    def x_store(state, at, s, level, rows):
        for f in range(F):
            state[at, s, 64 * f + 16 * level : 64 * f + 16 * level + 16] = rows[
                16 * f : 16 * f + 16
            ]

    here = (1, 2, 3, 5, 6, 7)
    for n in range(NT - 1):
        for k, value in zip(here, coarse(op_c, bc, [y[k, n] for k in here])):
            y[k, n + 1] = value

    def node(target, source, k, level=None, slices=None):
        slices = range(NT) if slices is None else slices
        low, high = EYZ * slices[0], EYZ * (slices[-1] + 1)

        def load(b):
            gather(b, source, k + 1, x_face(source, k, 3), x_face(source, k + 2, 0), slices)

        def run(b):
            if level is None:
                product = dot(op_r[...], b[:, low:high])
            else:
                product = dot((lo_op if level == 0 else up_op)[...], b[:, low:high])
            for j, s in enumerate(slices):
                if level is None:
                    target[k, s] = source[k + 1, s] + lanes_of(product, j)
                else:
                    x_store(
                        target, k, s, level, x_rows(source[k + 1, s], level) + lanes_of(product, j)
                    )

        return load, run

    def first(k):
        return node(u1, y, k, {0: 3, 6: 0}.get(k))

    def second(k, *rest):
        return node(u2, u1, k, *rest)

    tasks = [
        first(0),
        first(1),
        first(2),
        first(3),
        second(0, None, range(2)),
        second(0, 3, range(2, 4)),
        first(4),
        second(1),
        first(5),
        second(2),
        first(6),
        second(3),
        second(4, None, range(2)),
        second(4, 0, range(2, 4)),
    ]
    buffers = (b0, b1)
    tasks[0][0](b0)
    for i, (_, run) in enumerate(tasks):
        if i + 1 < len(tasks):
            tasks[i + 1][0](buffers[(i + 1) % 2])
        run(buffers[i % 2])

    for k in range(5):
        yp[k, 0] = y[k + 2, 0]
        yp[k, 1] = u2[k, 0]
    for n in (1, 2):
        change = coarse(op_c, bc, [yp[k, n] - y[k + 2, n] for k in range(5)])
        for k in range(5):
            if n == 2 and k in (0, 4):
                level = 3 if k == 0 else 0
                x_store(
                    yp, k, n + 1, level, x_rows(u2[k, n], level) + x_rows(change[k], level)
                )
            else:
                yp[k, n + 1] = u2[k, n] + change[k]

    for k in range(1, 4):
        for s in range(NT):
            w[k, s] = (5.0 / 12.0) * yp[k, s] + (2.0 / 3.0) * u1[k + 1, s] - (1.0 / 12.0) * u2[k, s]
    for k, level in ((0, 3), (4, 0)):
        for s in range(NT):
            x_store(
                w,
                k,
                s,
                level,
                (5.0 / 12.0) * x_rows(yp[k, s], level)
                + (2.0 / 3.0) * x_rows(u1[k + 1, s], level)
                - (1.0 / 12.0) * x_rows(u2[k, s], level),
            )

    def combine(start, one, two, product):
        return (1.0 / 3.0) * (start + one + two) + (start + product)

    sides = []
    gather(b0, w, 1, x_face(w, 0, 3), x_face(w, 2, 0))
    gather(b1, w, 3, x_face(w, 2, 3), x_face(w, 4, 0))
    product = dot(up_op[...], b0[...])
    for at, level, b, op in ((1, 3, b0, up_op), (3, 0, b1, lo_op)):
        product = dot(op[...], b[...])
        sides.append(
            [
                combine(
                    x_rows(yp[at, s], level),
                    x_rows(u1[at + 1, s], level),
                    x_rows(u2[at, s], level),
                    lanes_of(product, s),
                )
                for s in range(NT)
            ]
        )
    gather(b0, w, 2, x_face(w, 1, 3), x_face(w, 3, 0))
    product = dot(op_r[...], b0[...])
    for s in range(NT):
        w[2, s] = combine(yp[2, s], u1[3, s], u2[2, s], lanes_of(product, s))
    gather(b1, w, 2, lambda s: sides[0][s], lambda s: sides[1][s])
    product = dot(op_r[...], b1[...])
    last = [yp[2, s] + lanes_of(product, s) for s in range(NT)]

    begin = [y[HALO, 0], last[0]]
    for n in (1, 2):
        begin.append(last[n] + coarse(op_c, bc, [begin[n] - yp[2, n]])[0])

    @pl.when(core == 0)
    def _():
        for k in range(2):
            starts[k] = begin[k]
            ends[k] = last[k]

    @pl.when(core == 1)
    def _():
        for k in range(2):
            starts[k] = begin[2 + k]
            ends[k] = last[2 + k]


VMEM = pl.BlockSpec(memory_space=pltpu.VMEM)
LIMIT = pltpu.CompilerParams(vmem_limit_bytes=48 << 20)


def ready_made(own, far, volume, faces, rate):
    return pl.pallas_call(
        prepare,
        out_shape=(
            jax.ShapeDtypeStruct((FP, 3 * KR), BF),
            jax.ShapeDtypeStruct((FP, 3 * FP), BF),
            jax.ShapeDtypeStruct((3, NT, FP, EYZ), F32),
        ),
        in_specs=[VMEM] * 5,
        out_specs=(VMEM,) * 3,
        scratch_shapes=[pltpu.VMEM((3 * FP, 3 * EYZ), BF)],
        compiler_params=pltpu.CompilerParams(vmem_limit_bytes=24 << 20),
        cost_estimate=pl.CostEstimate(
            flops=4 * 10**9, bytes_accessed=6 * 10**6, transcendentals=0
        ),
        name="prepare",
    )(own, far, volume, faces, rate)


def work(where, ready, near, op_r, op_c):
    out = jax.ShapeDtypeStruct((2, FP, EYZ), F32)
    return pl.pallas_call(
        sweeps,
        out_shape=(out, out),
        in_specs=[pl.BlockSpec(memory_space=pltpu.SMEM)] + [VMEM] * 4,
        out_specs=(VMEM, VMEM),
        scratch_shapes=[
            pltpu.VMEM((WIN, NT, FP, EYZ), F32),
            pltpu.VMEM((7, NT, FP, EYZ), F32),
            pltpu.VMEM((5, NT, FP, EYZ), F32),
            pltpu.VMEM((5, NT, FP, EYZ), F32),
            pltpu.VMEM((5, NT, FP, EYZ), F32),
            pltpu.VMEM((3 * KR, NT * EYZ), BF),
            pltpu.VMEM((3 * KR, NT * EYZ), BF),
            pltpu.VMEM((3 * FP, 6 * EYZ), BF),
            pltpu.VMEM((FACE, 3 * KR), BF),
            pltpu.VMEM((FACE, 3 * KR), BF),
        ],
        compiler_params=LIMIT,
        name="sweeps",
    )(where, ready, near, op_r, op_c)


def pairs(mate_of, spaces):
    groups = []
    for core in range(2):
        for place in range(spaces):
            mate = mate_of(core, place)
            assert mate_of(core, mate) == place
            if place < mate:
                groups.append([core * spaces + place, core * spaces + mate])
    return groups


def swapped(block, mate_of, spaces):
    both = lax.all_gather(block, ("tm", "space"), axis_index_groups=pairs(mate_of, spaces))
    core, place = lax.axis_index("tm"), lax.axis_index("space")
    mate = mate_of(core, place)
    return jnp.where(mate > place, both[1], both[0])


def sent(block, mate_of, spaces):
    route = [route for a, b in pairs(mate_of, spaces) for route in ((a, b), (b, a))]
    return lax.ppermute(block, ("tm", "space"), route)


def other_row(spaces):
    def mate_of(core, place):
        down = (place // ROW + core) % 2
        return (place + ROW - 2 * ROW * down + spaces) % spaces

    return mate_of


def row_near(core, place):
    base, col = place // ROW * ROW, place % ROW
    return base + (1 - core) * (col + 1 - 2 * (col % 2)) + core * (ROW - 1 - col)


def row_far(core, place):
    return place // ROW * ROW + (place % ROW + 2) % ROW


def per_device(initial_state, volume_block, face_blocks, coarse_rate):
    spaces = lax.axis_size("space")
    core, place = lax.axis_index("tm"), lax.axis_index("space")
    col, odd_row = place % ROW, place // ROW % 2
    own = initial_state[0]

    across = swapped(own, other_row(spaces), spaces)
    far = lax.all_gather(across, "tm")
    above, below = far[odd_row], far[1 - odd_row]

    distant = sent(jnp.where(core == 0, own, jnp.where(col < 2, above, below)), row_far, spaces)
    gives_above = jnp.where(core == 0, col % 2 == 0, col < 2)
    close = sent(
        jnp.concatenate([own, jnp.where(gives_above, above, below)], axis=0), row_near, spaces
    )
    faces = jnp.transpose(face_blocks, (0, 2, 1)).reshape(6 * FACE, FP)
    op_r, op_c, ready = ready_made(own, far, volume_block, faces, coarse_rate)
    near = lax.all_gather(jnp.concatenate([close, distant], axis=0), "tm")

    where = jnp.stack([core, col, odd_row]).astype(jnp.int32)
    starts, ends = work(where, ready, near, op_r, op_c)
    return starts[:, None], ends[:, None]


def solution(mesh):
    return jax.shard_map(
        per_device,
        mesh=mesh,
        in_specs=(P("space", None, None), P(), P(), P()),
        out_specs=(P("tm", "space", None, None), P("tm", "space", None, None)),
        check_vma=False,
    )
```

time: 73.4 us -> 56.9 us (0.78)
  blocking collectives: 37.2 us -> 21 us
  starting transfers between devices: 0 us -> 7.42 us
  local copies, waits for them, and re-layouts: 5.78 us -> 0.02 us
  Pallas kernels: 27.7 us -> 23.1 us
  waiting for transfers between devices: 0 us -> 3.17 us
    all_gather x3 -> x1, blocking collectives: 32 us -> 16.3 us  [swapped(): lax.all_gather(block, ('tm', 'space'), axis_index_groups=pairs(mate_of, s...]
    ppermute x0 -> x2, starting transfers between devices: none -> 7.42 us  [sent(): return lax.ppermute(block, ('tm', 'space'), route)]
    pallas_call x1 -> x2, Pallas kernels: 27.7 us -> 23.1 us  [the longest x1 20.1 us: work(): pl.pallas_call(sweeps, out_shape=(out, out), in_specs=[pl.BlockSpec(memor...]
    concatenate x2 -> x0, local copies, waits for them, and re-layouts: 4.38 us -> none  [the longest x1 2.9 us: operator(): return jnp.concatenate([high, low, high], axis=1).astype(BF)]
    ppermute x0 -> x2, waiting for transfers between devices: none -> 3.17 us  [sent(): return lax.ppermute(block, ('tm', 'space'), route)]
    unnamed x12 -> x8, local copies, waits for them, and re-layouts: 1.35 us -> 0.02 us
    another operation x2 -> x0, other arithmetic: 1.27 us -> none
    select_n x0 -> x1, other arithmetic: none -> 0.94 us  [per_device(): jnp.where(core == 0, own, jnp.where(col < 2, above, below))]
  transfers between devices with their start and end apart: 0 -> 2, of which waited for: 0 -> 1; matrix products, arithmetic and copies ran while one was open for 0% -> 0% of each run, Pallas kernels for 0% -> 5%
where the time goes in v2:
time: 56.9 us; the launch traced here: 56.7 us
  Pallas kernels  23.1 us (41%)
  blocking collectives  21 us (37%)
  starting transfers between devices  7.42 us (13%)
  waiting for transfers between devices  3.17 us (6%)
  other arithmetic  1.12 us (2%)
  between operations  0.85 us (1%)
    pallas_call x1, Pallas kernels, work(): pl.pallas_call(sweeps, out_shape=(out, out), in_specs=[pl.BlockSpec(memor...  20.1 us
    all_gather x1, blocking collectives, swapped(): lax.all_gather(block, ('tm', 'space'), axis_index_groups=pairs(mate_of, s...  16.3 us
    ppermute x2, starting transfers between devices, sent(): return lax.ppermute(block, ('tm', 'space'), route)  7.42 us
    ppermute x2, waiting for transfers between devices, sent(): return lax.ppermute(block, ('tm', 'space'), route)  3.17 us
    pallas_call x1, Pallas kernels, ready_made(): pl.pallas_call(prepare, out_shape=(jax.ShapeDtypeStruct((FP, 3 * KR), BF)...  2.96 us
    all_gather x1, blocking collectives, per_device(): near = lax.all_gather(jnp.concatenate([close, distant], axis=0), 'tm')  2.69 us
    all_gather x1, blocking collectives, per_device(): far = lax.all_gather(across, 'tm')  2.04 us
  transfers between devices with their start and end apart: 2, of which 1 were waited for; matrix products, arithmetic and copies ran while one was open for 0% of the time, Pallas kernels for 5%

profile of v2, /device:TPU:1, one launch (start us, length us, event | category | flops | bytes accessed | tf_op | source)
XLA Modules:
  0.0 56.7 jit_solution(4063786361969039206)
XLA Ops:
  0.6 0.0 copy-start
  0.6 0.0 copy-start.3
  0.7 0.0 copy-start.1
  0.7 0.0 copy-start.2
  0.8 16.3 %all_gather.13 = f32[2,320,128]{2,1,0:T(8,128)S(1)} all-gather(f32[1,320,128]{2,1,0:T(8,128)} %param.4), channel_id=1, replica_groups={{0,4},{1,5},{2,6},{3,7},{8,12},{9,13},{10,14},{11,15},{16,20},{17,21},{..., dimensions={0}, use_global_device_ids=true | all-gather | bytes 491520 | tf_op jit(solution)/shard_map/all_gather | solution.py:351
  17.0 2.0 %all_gather.14.far = f32[2,320,128]{2,1,0:T(8,128)S(1)} all-gather(f32[1,320,128]{2,1,0:T(8,128)S(1)} %slice_select_fusion), channel_id=1, replica_groups=mesh['tm'=2,'space'=256] {'tm'}, dimensions={0}, use_global_device_ids=true | all-gather | bytes 491520 | tf_op jit(solution)/shard_map/all_gather | solution.py:386
  19.1 0.9 %bitcast_select_fusion = f32[320,128]{1,0:T(8,128)S(1)} fusion(f32[2,320,128]{2,1,0:T(8,128)S(1)} %all_gather.14.far, s32[]{:T(128)S(6)} %select_n.82, s32[]{:T(128)S(6)} %select_n.81, pred[]{:T(512)S(6)} %lt.37, pred[]{:T(512)S(6)} %eq.13, f32[1,320,128]{2,1,0:T(8,128)} %param.4), kind=kLoop, calls=%fused_computation.3 | loop fusion | flops 81920 | bytes 655370 | tf_op jit(solution)/shard_map/jit(_where)/select_n | solution.py:389
  20.0 4.7 %collective-permute-start.1 = (f32[320,128]{1,0:T(8,128)S(1)}, f32[320,128]{1,0:T(8,128)S(1)}, u32[]{:S(2)}, u32[]{:S(2)}) collective-permute-start(f32[320,128]{1,0:T(8,128)S(1)} %bitcast_select_fusion), channel_id=1, source_target_pairs={{0,2},{2,0},{1,3},{3,1},{4,6},{6,4},{5,7},{7,5},{8,10},{10,8},{9,1... | collective-permute-start | bytes 491528 | tf_op jit(solution)/shard_map/ppermute | solution.py:359
  24.7 0.0 copy-done
  24.8 2.8 %collective-permute-start = (f32[640,128]{1,0:T(8,128)S(1)}, f32[640,128]{1,0:T(8,128)S(1)}, u32[]{:S(2)}, u32[]{:S(2)}) collective-permute-start(f32[640,128]{1,0:T(8,128)S(1)} %pad_maximum_fusion.1), channel_id=1, source_target_pairs={{0,1},{1,0},{2,3},{3,2},{4,5},{5,4},{6,7},{7,6},{8,9},{9,8},{10,11... | collective-permute-start | bytes 983048 | tf_op jit(solution)/shard_map/ppermute | solution.py:359
  27.6 0.0 copy-done.3
  27.6 0.0 copy-done.1
  27.6 0.0 copy-done.2
  27.6 3.0 %prepare.1 = (bf16[320,2400]{1,0:T(8,128)(2,1)S(1)}, bf16[320,960]{1,0:T(8,128)(2,1)S(1)}, f32[3,4,320,128]{3,2,1,0:T(8,128)S(1)}) custom-call(f32[320,128]{1,0:T(8,128)S(1)} %bitcast.21, f32[2,320,128]{2,1,0:T(8,128)S(1)} %all_gather.14.far, f32[320,320]{1,0:T(8,128)S(1)} %copy-done.2, f32[480,320]{1,0:T(8,128)S(1)} %bitcast.22, f32[320,320]{1,0:T(8,128)S(1)} %copy-done.3), custom_call_target="tpu_custom_call" | custom-call | flops 4000000000 | bytes 6000000 | tf_op jit(solution)/shard_map/prepare/pallas_call | solution.py:297
  30.6 0.1 pad_add_fusion.where
  30.6 0.0 collective-permute-done.1
  30.6 3.2 %collective-permute-done = f32[640,128]{1,0:T(8,128)S(1)} collective-permute-done((f32[640,128]{1,0:T(8,128)S(1)}, f32[640,128]{1,0:T(8,128)S(1)}, u32[]{:S(2)}, u32[]{:S(2)}) %collective-permute-start) | collective-permute-done | bytes 327712 | tf_op jit(solution)/shard_map/ppermute | solution.py:359
  33.9 2.7 %all-gather = f32[1920,128]{1,0:T(8,128)S(1)} all-gather(f32[960,128]{1,0:T(8,128)S(1)} %pad_maximum_fusion), channel_id=2, replica_groups=mesh['tm'=2,'space'=256] {'tm'}, dimensions={0}, use_global_device_ids=true | all-gather | bytes 1474560 | tf_op jit(solution)/shard_map/all_gather | solution.py:396
  36.6 20.1 %sweeps.1 = (f32[2,320,128]{2,1,0:T(8,128)}, f32[2,320,128]{2,1,0:T(8,128)}) custom-call(s32[3]{0:T(128)S(1)} %pad_add_fusion.where, f32[3,4,320,128]{3,2,1,0:T(8,128)S(1)} %get-tuple-element.7.ready, f32[2,960,128]{2,1,0:T(8,128)S(1)} %bitcast.19, bf16[320,2400]{1,0:T(8,128)(2,1)S(1)} %get-tuple-element.8.op_r, bf16[320,960]{1,0:T(8,128)(2,1)S(1)} %get-tuple-element.9.op_c), custom_call_target="tpu_custom_call" | custom-call | tf_op jit(solution)/shard_map/sweeps/pallas_call | solution.py:317
  (4 shorter events, 0.1 us)
Async XLA Ops:
  0.6 24.1 %copy-start = (f32[1,320,128]{2,1,0:T(8,128)S(1)}, f32[1,320,128]{2,1,0:T(8,128)}, u32[]{:S(2)}) copy-start(f32[1,320,128]{2,1,0:T(8,128)} %param.4) | copy-start | bytes 491524
  0.6 26.9 %copy-start.3 = (f32[320,320]{1,0:T(8,128)S(1)}, f32[320,320]{1,0:T(8,128)}, u32[]{:S(2)}) copy-start(f32[320,320]{1,0:T(8,128)} %rate.1) | copy-start | bytes 1228804
  0.7 26.9 %copy-start.1 = (f32[6,320,80]{1,2,0:T(8,128)S(1)}, f32[6,320,80]{1,2,0:T(8,128)}, u32[]{:S(2)}) copy-start(f32[6,320,80]{1,2,0:T(8,128)} %param.6) | copy-start | bytes 1843204
  0.7 26.9 %copy-start.2 = (f32[320,320]{1,0:T(8,128)S(1)}, f32[320,320]{1,0:T(8,128)}, u32[]{:S(2)}) copy-start(f32[320,320]{1,0:T(8,128)} %volume.1) | copy-start | bytes 1228804
  20.0 10.6 %collective-permute-start.1 = (f32[320,128]{1,0:T(8,128)S(1)}, f32[320,128]{1,0:T(8,128)S(1)}, u32[]{:S(2)}, u32[]{:S(2)}) collective-permute-start(f32[320,128]{1,0:T(8,128)S(1)} %bitcast_select_fusion), channel_id=1, source_target_pairs={{0,2},{2,0},{1,3},{3,1},{4,6},{6,4},{5,7},{7,5},{8,10},{10,8},{9,1... | collective-permute-start | bytes 491528 | tf_op jit(solution)/shard_map/ppermute | solution.py:359
  24.8 9.0 %collective-permute-start = (f32[640,128]{1,0:T(8,128)S(1)}, f32[640,128]{1,0:T(8,128)S(1)}, u32[]{:S(2)}, u32[]{:S(2)}) collective-permute-start(f32[640,128]{1,0:T(8,128)S(1)} %pad_maximum_fusion.1), channel_id=1, source_target_pairs={{0,1},{1,0},{2,3},{3,2},{4,5},{5,4},{6,7},{7,6},{8,9},{9,8},{10,11... | collective-permute-start | bytes 983048 | tf_op jit(solution)/shard_map/ppermute | solution.py:359

commit v3 on v2

--- a/solution.py
+++ b/solution.py
@@ -78,7 +78,40 @@
     return [value + lanes_of(product, k) for k, value in enumerate(values)]
 
 
-def prepare(own, far, volume, faces, rate, op_r, op_c, y, bc):
+def put(b, base, lanes, value):
+    rows = value.shape[0]
+    whole = min(rows, MAIN - base)
+    high, low = split(value)
+    for k, part in enumerate((high, high, low)):
+        b[MAIN * k + base : MAIN * k + base + whole, lanes] = part[:whole]
+        if whole < rows:
+            b[3 * MAIN + REST * k : 3 * MAIN + REST * (k + 1), lanes] = part[whole:]
+
+
+def gather(b, state, at, minus_x, plus_x, slices=range(NT)):
+    lane = lax.broadcasted_iota(jnp.int32, (FACE, EYZ), 1) % EZ
+    for s in slices:
+        lanes = slice(EYZ * s, EYZ * (s + 1))
+        value = state[at, s]
+        put(b, 0, lanes, value)
+        if minus_x is not None:
+            put(b, FP, lanes, minus_x(s))
+            put(b, FP + FACE, lanes, plus_x(s))
+        put(b, FP + 2 * FACE, lanes, pltpu.roll(y_face(value, 3), EZ, 1))
+        put(b, FP + 3 * FACE, lanes, pltpu.roll(y_face(value, 0), EYZ - EZ, 1))
+        low_z = state[at, s, pl.ds(3, FACE, stride=4), :]
+        high_z = state[at, s, pl.ds(0, FACE, stride=4), :]
+        low_z = jnp.where(
+            lane == 0, pltpu.roll(low_z, EYZ - EZ + 1, 1), pltpu.roll(low_z, 1, 1)
+        )
+        high_z = jnp.where(
+            lane == EZ - 1, pltpu.roll(high_z, EZ - 1, 1), pltpu.roll(high_z, EYZ - 1, 1)
+        )
+        put(b, FP + 4 * FACE, lanes, low_z)
+        put(b, FP + 5 * FACE, lanes, high_z)
+
+
+def prepare(own, far, volume, faces, rate, op_r, op_x, op_c, y, part, bc, b):
     step = 0.25
     side_by_side(op_c, *split(step * rate[...]), CMAIN, CREST)
     for k, start in enumerate((own[...], far[0], far[1])):
@@ -98,10 +131,20 @@
         (dot(v, here) + dot_first(f, there)).astype(BF) for v, f in zip(volumes, fluxes)
     ]
     side_by_side(op_r, high, low, MAIN, REST)
-
-
-def sweeps(where, ready, near, op_r, op_c, starts, ends, y, u1, u2, yp, w, b0, b1, bc, up_op, lo_op):
-    core, col, odd_row = where[0], where[1], where[2]
+    for k, columns in enumerate((high, low, high)):
+        op_x[:, 2 * FACE * k : 2 * FACE * (k + 1)] = columns[:, FP : FP + 2 * FACE]
+
+    gather(b, y, 0, None, None)
+    for k in range(3):
+        b[MAIN * k + FP : MAIN * k + FP + 2 * FACE] = jnp.zeros((2 * FACE, NT * EYZ), BF)
+    product = dot(op_r[...], b[...])
+    for s in range(NT):
+        part[s] = y[0, s] + lanes_of(product, s)
+
+
+def sweeps(ready, part, near, op_r, op_x, op_c, starts, ends, y, u1, u2, yp, w, b0, b1, bx, bc, up_op, lo_op):
+    core, place_here = lax.axis_index("tm"), lax.axis_index("space")
+    col, odd_row = lax.rem(place_here, ROW), lax.rem(lax.div(place_here, ROW), 2)
 
     def place(mate, own_block, other_block):
         y[mate - col + HALO, 0] = own_block
@@ -118,37 +161,6 @@
     for f in range(F):
         up_op[16 * f : 16 * f + 16] = op_r[64 * f + 48 : 64 * f + 64]
         lo_op[16 * f : 16 * f + 16] = op_r[64 * f : 64 * f + 16]
-
-    lane = lax.broadcasted_iota(jnp.int32, (FACE, EYZ), 1) % EZ
-
-    def put(b, base, lanes, value):
-        rows = value.shape[0]
-        whole = min(rows, MAIN - base)
-        high, low = split(value)
-        for k, part in enumerate((high, high, low)):
-            b[MAIN * k + base : MAIN * k + base + whole, lanes] = part[:whole]
-            if whole < rows:
-                b[3 * MAIN + REST * k : 3 * MAIN + REST * (k + 1), lanes] = part[whole:]
-
-    def gather(b, state, at, minus_x, plus_x, slices=range(NT)):
-        for s in slices:
-            lanes = slice(EYZ * s, EYZ * (s + 1))
-            value = state[at, s]
-            put(b, 0, lanes, value)
-            put(b, FP, lanes, minus_x(s))
-            put(b, FP + FACE, lanes, plus_x(s))
-            put(b, FP + 2 * FACE, lanes, pltpu.roll(y_face(value, 3), EZ, 1))
-            put(b, FP + 3 * FACE, lanes, pltpu.roll(y_face(value, 0), EYZ - EZ, 1))
-            low_z = state[at, s, pl.ds(3, FACE, stride=4), :]
-            high_z = state[at, s, pl.ds(0, FACE, stride=4), :]
-            low_z = jnp.where(
-                lane == 0, pltpu.roll(low_z, EYZ - EZ + 1, 1), pltpu.roll(low_z, 1, 1)
-            )
-            high_z = jnp.where(
-                lane == EZ - 1, pltpu.roll(high_z, EZ - 1, 1), pltpu.roll(high_z, EYZ - 1, 1)
-            )
-            put(b, FP + 4 * FACE, lanes, low_z)
-            put(b, FP + 5 * FACE, lanes, high_z)
 
     def x_face(state, at, level):
         return lambda s: x_rows(state[at, s], level)
@@ -186,6 +198,23 @@
 
         return load, run
 
+    def first_here():
+        def load(b):
+            for s in range(NT):
+                lanes = slice(EYZ * s, EYZ * (s + 1))
+                for j, rows in enumerate((x_rows(y[HALO - 1, s], 3), x_rows(y[HALO + 1, s], 0))):
+                    high, low = split(rows)
+                    for k, piece in enumerate((high, high, low)):
+                        at = 2 * FACE * k + FACE * j
+                        bx[at : at + FACE, lanes] = piece
+
+        def run(b):
+            product = dot(op_x[...], bx[...])
+            for s in range(NT):
+                u1[3, s] = part[s] + lanes_of(product, s)
+
+        return load, run
+
     def first(k):
         return node(u1, y, k, {0: 3, 6: 0}.get(k))
 
@@ -196,7 +225,7 @@
         first(0),
         first(1),
         first(2),
-        first(3),
+        first_here(),
         second(0, None, range(2)),
         second(0, 3, range(2, 4)),
         first(4),
@@ -298,12 +327,17 @@
         prepare,
         out_shape=(
             jax.ShapeDtypeStruct((FP, 3 * KR), BF),
+            jax.ShapeDtypeStruct((FP, 6 * FACE), BF),
             jax.ShapeDtypeStruct((FP, 3 * FP), BF),
             jax.ShapeDtypeStruct((3, NT, FP, EYZ), F32),
+            jax.ShapeDtypeStruct((NT, FP, EYZ), F32),
         ),
         in_specs=[VMEM] * 5,
-        out_specs=(VMEM,) * 3,
-        scratch_shapes=[pltpu.VMEM((3 * FP, 3 * EYZ), BF)],
+        out_specs=(VMEM,) * 5,
+        scratch_shapes=[
+            pltpu.VMEM((3 * FP, 3 * EYZ), BF),
+            pltpu.VMEM((3 * KR, NT * EYZ), BF),
+        ],
         compiler_params=pltpu.CompilerParams(vmem_limit_bytes=24 << 20),
         cost_estimate=pl.CostEstimate(
             flops=4 * 10**9, bytes_accessed=6 * 10**6, transcendentals=0
@@ -312,12 +346,12 @@
     )(own, far, volume, faces, rate)
 
 
-def work(where, ready, near, op_r, op_c):
+def work(ready, part, near, op_r, op_x, op_c):
     out = jax.ShapeDtypeStruct((2, FP, EYZ), F32)
     return pl.pallas_call(
         sweeps,
         out_shape=(out, out),
-        in_specs=[pl.BlockSpec(memory_space=pltpu.SMEM)] + [VMEM] * 4,
+        in_specs=[VMEM] * 6,
         out_specs=(VMEM, VMEM),
         scratch_shapes=[
             pltpu.VMEM((WIN, NT, FP, EYZ), F32),
@@ -327,13 +361,14 @@
             pltpu.VMEM((5, NT, FP, EYZ), F32),
             pltpu.VMEM((3 * KR, NT * EYZ), BF),
             pltpu.VMEM((3 * KR, NT * EYZ), BF),
+            pltpu.VMEM((6 * FACE, NT * EYZ), BF),
             pltpu.VMEM((3 * FP, 6 * EYZ), BF),
             pltpu.VMEM((FACE, 3 * KR), BF),
             pltpu.VMEM((FACE, 3 * KR), BF),
         ],
         compiler_params=LIMIT,
         name="sweeps",
-    )(where, ready, near, op_r, op_c)
+    )(ready, part, near, op_r, op_x, op_c)
 
 
 def pairs(mate_of, spaces):
@@ -350,8 +385,8 @@
 def swapped(block, mate_of, spaces):
     both = lax.all_gather(block, ("tm", "space"), axis_index_groups=pairs(mate_of, spaces))
     core, place = lax.axis_index("tm"), lax.axis_index("space")
-    mate = mate_of(core, place)
-    return jnp.where(mate > place, both[1], both[0])
+    first = mate_of(core, place) > place
+    return jnp.where(first, both[1], both[0]), jnp.where(first, both[0], both[1])
 
 
 def sent(block, mate_of, spaces):
@@ -382,7 +417,7 @@
     col, odd_row = place % ROW, place // ROW % 2
     own = initial_state[0]
 
-    across = swapped(own, other_row(spaces), spaces)
+    across, own = swapped(own, other_row(spaces), spaces)
     far = lax.all_gather(across, "tm")
     above, below = far[odd_row], far[1 - odd_row]
 
@@ -392,11 +427,10 @@
         jnp.concatenate([own, jnp.where(gives_above, above, below)], axis=0), row_near, spaces
     )
     faces = jnp.transpose(face_blocks, (0, 2, 1)).reshape(6 * FACE, FP)
-    op_r, op_c, ready = ready_made(own, far, volume_block, faces, coarse_rate)
+    op_r, op_x, op_c, ready, part = ready_made(own, far, volume_block, faces, coarse_rate)
     near = lax.all_gather(jnp.concatenate([close, distant], axis=0), "tm")
 
-    where = jnp.stack([core, col, odd_row]).astype(jnp.int32)
-    starts, ends = work(where, ready, near, op_r, op_c)
+    starts, ends = work(ready, part, near, op_r, op_x, op_c)
     return starts[:, None], ends[:, None]
 
 

time: 56.9 us -> 54.7 us (0.961)
  other arithmetic: 1.12 us -> 0.14 us
  waiting for transfers between devices: 3.17 us -> 2.23 us
    pallas_call x1, Pallas kernels: 20.1 us -> 18.9 us  [work(): pl.pallas_call(sweeps, out_shape=(out, out), in_specs=[VMEM] * 6, out_spe...]
    pallas_call x1, Pallas kernels: 2.96 us -> 3.98 us  [ready_made(): pl.pallas_call(prepare, out_shape=(jax.ShapeDtypeStruct((FP, 3 * KR), BF)...]
    ppermute x2, waiting for transfers between devices: 3.17 us -> 2.23 us  [sent(): return lax.ppermute(block, ('tm', 'space'), route)]
    select_n x1, other arithmetic: 0.94 us -> 0.04 us  [per_device(): jnp.where(core == 0, own, jnp.where(col < 2, above, below))]
  transfers between devices with their start and end apart: 2 -> 2, of which waited for: 1 -> 1; matrix products, arithmetic and copies ran while one was open for 0% -> 0% of each run, Pallas kernels for 5% -> 7%
where the time goes in v3:
time: 54.7 us; the launch traced here: 54.5 us
  Pallas kernels  22.9 us (42%)
  blocking collectives  21 us (38%)
  starting transfers between devices  7.42 us (14%)
  waiting for transfers between devices  2.23 us (4%)
  between operations  0.84 us (2%)
    pallas_call x1, Pallas kernels, work(): pl.pallas_call(sweeps, out_shape=(out, out), in_specs=[VMEM] * 6, out_spe...  18.9 us
    all_gather x1, blocking collectives, swapped(): lax.all_gather(block, ('tm', 'space'), axis_index_groups=pairs(mate_of, s...  16.3 us
    ppermute x2, starting transfers between devices, sent(): return lax.ppermute(block, ('tm', 'space'), route)  7.42 us
    pallas_call x1, Pallas kernels, ready_made(): pl.pallas_call(prepare, out_shape=(jax.ShapeDtypeStruct((FP, 3 * KR), BF)...  3.98 us
    all_gather x1, blocking collectives, per_device(): near = lax.all_gather(jnp.concatenate([close, distant], axis=0), 'tm')  2.69 us
    ppermute x2, waiting for transfers between devices, sent(): return lax.ppermute(block, ('tm', 'space'), route)  2.23 us
    all_gather x1, blocking collectives, per_device(): far = lax.all_gather(across, 'tm')  2.04 us
  transfers between devices with their start and end apart: 2, of which 1 were waited for; matrix products, arithmetic and copies ran while one was open for 0% of the time, Pallas kernels for 7%

profile of v3, /device:TPU:1, one launch (start us, length us, event | category | flops | bytes accessed | tf_op | source)
XLA Modules:
  0.0 54.5 jit_solution(8456545148885467199)
XLA Ops:
  0.6 0.0 copy-start.2
  0.6 0.0 copy-start
  0.7 0.0 copy-start.1
  0.7 16.3 %all_gather.13 = f32[2,320,128]{2,1,0:T(8,128)S(1)} all-gather(f32[1,320,128]{2,1,0:T(8,128)} %param.4), channel_id=1, replica_groups={{0,4},{1,5},{2,6},{3,7},{8,12},{9,13},{10,14},{11,15},{16,20},{17,21},{..., dimensions={0}, use_global_device_ids=true | all-gather | bytes 491520 | tf_op jit(solution)/shard_map/all_gather | solution.py:386
  17.0 2.0 %all_gather.14.far = f32[2,320,128]{2,1,0:T(8,128)S(1)} all-gather(f32[1,320,128]{2,1,0:T(8,128)S(1)} %slice_select_fusion), channel_id=1, replica_groups=mesh['tm'=2,'space'=256] {'tm'}, dimensions={0}, use_global_device_ids=true | all-gather | bytes 491520 | tf_op jit(solution)/shard_map/all_gather | solution.py:421
  19.1 4.7 %collective-permute-start.1 = (f32[320,128]{1,0:T(8,128)S(1)}, f32[320,128]{1,0:T(8,128)S(1)}, u32[]{:S(2)}, u32[]{:S(2)}) collective-permute-start(f32[320,128]{1,0:T(8,128)S(1)} %get-tuple-element.20), channel_id=1, source_target_pairs={{0,2},{2,0},{1,3},{3,1},{4,6},{6,4},{5,7},{7,5},{8,10},{10,8},{9,1... | collective-permute-start | bytes 491528 | tf_op jit(solution)/shard_map/ppermute | solution.py:394
  23.9 2.8 %collective-permute-start = (f32[640,128]{1,0:T(8,128)S(1)}, f32[640,128]{1,0:T(8,128)S(1)}, u32[]{:S(2)}, u32[]{:S(2)}) collective-permute-start(f32[640,128]{1,0:T(8,128)S(1)} %pad_maximum_fusion.1), channel_id=1, source_target_pairs={{0,1},{1,0},{2,3},{3,2},{4,5},{5,4},{6,7},{7,6},{8,9},{9,8},{10,11... | collective-permute-start | bytes 983048 | tf_op jit(solution)/shard_map/ppermute | solution.py:394
  26.6 0.0 copy-done.2
  26.6 0.0 copy-done
  26.7 0.0 copy-done.1
  26.7 4.0 %prepare.1 = (bf16[320,2400]{1,0:T(8,128)(2,1)S(1)}, bf16[320,480]{1,0:T(8,128)(2,1)S(1)}, bf16[320,960]{1,0:T(8,128)(2,1)S(1)}, f32[3,4,320,128]{3,2,1,0:T(8,128)S(1)}, f32[4,320,128]{2,1,0:T(8,128)S(1)}) custom-call(f32[320,128]{1,0:T(8,128)S(1)} %get-tuple-element.21.own, f32[2,320,128]{2,1,0:T(8,128)S(1)} %all_gather.14.far, f32[320,320]{1,0:T(8,128)S(1)} %copy-done.1, ...), custom_call_target="tpu_custom_call" | custom-call | flops 4000000000 | bytes 6000000 | tf_op jit(solution)/shard_map/prepare/pallas_call | solution.py:326
  30.7 0.0 collective-permute-done.1
  30.7 2.2 %collective-permute-done = f32[640,128]{1,0:T(8,128)S(1)} collective-permute-done((f32[640,128]{1,0:T(8,128)S(1)}, f32[640,128]{1,0:T(8,128)S(1)}, u32[]{:S(2)}, u32[]{:S(2)}) %collective-permute-start) | collective-permute-done | bytes 327712 | tf_op jit(solution)/shard_map/ppermute | solution.py:394
  32.9 2.7 %all-gather = f32[1920,128]{1,0:T(8,128)S(1)} all-gather(f32[960,128]{1,0:T(8,128)S(1)} %pad_maximum_fusion), channel_id=2, replica_groups=mesh['tm'=2,'space'=256] {'tm'}, dimensions={0}, use_global_device_ids=true | all-gather | bytes 1474560 | tf_op jit(solution)/shard_map/all_gather | solution.py:431
  35.6 18.9 %sweeps.1 = (f32[2,320,128]{2,1,0:T(8,128)}, f32[2,320,128]{2,1,0:T(8,128)}) custom-call(f32[3,4,320,128]{3,2,1,0:T(8,128)S(1)} %get-tuple-element.9.ready, f32[4,320,128]{2,1,0:T(8,128)S(1)} %get-tuple-element.10.part, f32[2,960,128]{2,1,0:T(8,128)S(1)} %bitcast.17, bf16[320,2400]{1,0:T(8,128)(2,1)S(1)} %get-tuple-element.11.op_r, ...), custom_call_target="tpu_custom_call" | custom-call | tf_op jit(solution)/shard_map/sweeps/pallas_call | solution.py:351
  (5 shorter events, 0.1 us)
Async XLA Ops:
  0.6 26.0 %copy-start.2 = (f32[320,320]{1,0:T(8,128)S(1)}, f32[320,320]{1,0:T(8,128)}, u32[]{:S(2)}) copy-start(f32[320,320]{1,0:T(8,128)} %rate.1) | copy-start | bytes 1228804
  0.6 26.0 %copy-start = (f32[6,320,80]{1,2,0:T(8,128)S(1)}, f32[6,320,80]{1,2,0:T(8,128)}, u32[]{:S(2)}) copy-start(f32[6,320,80]{1,2,0:T(8,128)} %param.6) | copy-start | bytes 1843204
  0.7 26.0 %copy-start.1 = (f32[320,320]{1,0:T(8,128)S(1)}, f32[320,320]{1,0:T(8,128)}, u32[]{:S(2)}) copy-start(f32[320,320]{1,0:T(8,128)} %volume.1) | copy-start | bytes 1228804
  19.1 11.5 %collective-permute-start.1 = (f32[320,128]{1,0:T(8,128)S(1)}, f32[320,128]{1,0:T(8,128)S(1)}, u32[]{:S(2)}, u32[]{:S(2)}) collective-permute-start(f32[320,128]{1,0:T(8,128)S(1)} %get-tuple-element.20), channel_id=1, source_target_pairs={{0,2},{2,0},{1,3},{3,1},{4,6},{6,4},{5,7},{7,5},{8,10},{10,8},{9,1... | collective-permute-start | bytes 491528 | tf_op jit(solution)/shard_map/ppermute | solution.py:394
  23.9 9.0 %collective-permute-start = (f32[640,128]{1,0:T(8,128)S(1)}, f32[640,128]{1,0:T(8,128)S(1)}, u32[]{:S(2)}, u32[]{:S(2)}) collective-permute-start(f32[640,128]{1,0:T(8,128)S(1)} %pad_maximum_fusion.1), channel_id=1, source_target_pairs={{0,1},{1,0},{2,3},{3,2},{4,5},{5,4},{6,7},{7,6},{8,9},{9,8},{10,11... | collective-permute-start | bytes 983048 | tf_op jit(solution)/shard_map/ppermute | solution.py:394

commit v4 on v3

--- a/solution.py
+++ b/solution.py
@@ -142,7 +142,7 @@
         part[s] = y[0, s] + lanes_of(product, s)
 
 
-def sweeps(ready, part, near, op_r, op_x, op_c, starts, ends, y, u1, u2, yp, w, b0, b1, bx, bc, up_op, lo_op):
+def sweeps(ready, part, near, op_r, op_x, op_c, starts, ends, y, u1, u2, yp, w, v, b0, b1, b2, b3, bx, bc, bd, up_op, lo_op):
     core, place_here = lax.axis_index("tm"), lax.axis_index("space")
     col, odd_row = lax.rem(place_here, ROW), lax.rem(lax.div(place_here, ROW), 2)
 
@@ -237,18 +237,21 @@
         second(4, None, range(2)),
         second(4, 0, range(2, 4)),
     ]
-    buffers = (b0, b1)
+    buffers = (b0, b1, b2, b3)
     tasks[0][0](b0)
+    tasks[1][0](b1)
     for i, (_, run) in enumerate(tasks):
-        if i + 1 < len(tasks):
-            tasks[i + 1][0](buffers[(i + 1) % 2])
-        run(buffers[i % 2])
+        if i + 2 < len(tasks) and i in (0, 1):
+            tasks[i + 2][0](buffers[(i + 2) % 4])
+        run(buffers[i % 4])
+        if i + 2 < len(tasks) and i not in (0, 1):
+            tasks[i + 2][0](buffers[(i + 2) % 4])
 
     for k in range(5):
         yp[k, 0] = y[k + 2, 0]
         yp[k, 1] = u2[k, 0]
     for n in (1, 2):
-        change = coarse(op_c, bc, [yp[k, n] - y[k + 2, n] for k in range(5)])
+        change = coarse(op_c, bd.at[n - 1], [yp[k, n] - y[k + 2, n] for k in range(5)])
         for k in range(5):
             if n == 2 and k in (0, 4):
                 level = 3 if k == 0 else 0
@@ -276,29 +279,28 @@
     def combine(start, one, two, product):
         return (1.0 / 3.0) * (start + one + two) + (start + product)
 
-    sides = []
-    gather(b0, w, 1, x_face(w, 0, 3), x_face(w, 2, 0))
-    gather(b1, w, 3, x_face(w, 2, 3), x_face(w, 4, 0))
-    product = dot(up_op[...], b0[...])
-    for at, level, b, op in ((1, 3, b0, up_op), (3, 0, b1, lo_op)):
+    def side(at, level, op, b):
         product = dot(op[...], b[...])
-        sides.append(
-            [
-                combine(
-                    x_rows(yp[at, s], level),
-                    x_rows(u1[at + 1, s], level),
-                    x_rows(u2[at, s], level),
-                    lanes_of(product, s),
-                )
-                for s in range(NT)
-            ]
-        )
+        return [
+            combine(
+                x_rows(yp[at, s], level),
+                x_rows(u1[at + 1, s], level),
+                x_rows(u2[at, s], level),
+                lanes_of(product, s),
+            )
+            for s in range(NT)
+        ]
+
     gather(b0, w, 2, x_face(w, 1, 3), x_face(w, 3, 0))
+    gather(b1, w, 1, x_face(w, 0, 3), x_face(w, 2, 0))
     product = dot(op_r[...], b0[...])
     for s in range(NT):
-        w[2, s] = combine(yp[2, s], u1[3, s], u2[2, s], lanes_of(product, s))
-    gather(b1, w, 2, lambda s: sides[0][s], lambda s: sides[1][s])
-    product = dot(op_r[...], b1[...])
+        v[0, s] = combine(yp[2, s], u1[3, s], u2[2, s], lanes_of(product, s))
+    gather(b2, w, 3, x_face(w, 2, 3), x_face(w, 4, 0))
+    below = side(1, 3, up_op, b1)
+    above = side(3, 0, lo_op, b2)
+    gather(b3, v, 0, lambda s: below[s], lambda s: above[s])
+    product = dot(op_r[...], b3[...])
     last = [yp[2, s] + lanes_of(product, s) for s in range(NT)]
 
     begin = [y[HALO, 0], last[0]]
@@ -359,10 +361,14 @@
             pltpu.VMEM((5, NT, FP, EYZ), F32),
             pltpu.VMEM((5, NT, FP, EYZ), F32),
             pltpu.VMEM((5, NT, FP, EYZ), F32),
+            pltpu.VMEM((1, NT, FP, EYZ), F32),
+            pltpu.VMEM((3 * KR, NT * EYZ), BF),
+            pltpu.VMEM((3 * KR, NT * EYZ), BF),
             pltpu.VMEM((3 * KR, NT * EYZ), BF),
             pltpu.VMEM((3 * KR, NT * EYZ), BF),
             pltpu.VMEM((6 * FACE, NT * EYZ), BF),
             pltpu.VMEM((3 * FP, 6 * EYZ), BF),
+            pltpu.VMEM((2, 3 * FP, 5 * EYZ), BF),
             pltpu.VMEM((FACE, 3 * KR), BF),
             pltpu.VMEM((FACE, 3 * KR), BF),
         ],

time: 54.7 us -> 53.6 us (0.980)
  Pallas kernels: 22.9 us -> 21.8 us
    pallas_call x1, Pallas kernels: 18.9 us -> 17.8 us  [work(): pl.pallas_call(sweeps, out_shape=(out, out), in_specs=[VMEM] * 6, out_spe...]
where the time goes in v4:
time: 53.6 us; the launch traced here: 53.5 us
  Pallas kernels  21.8 us (41%)
  blocking collectives  21 us (39%)
  starting transfers between devices  7.42 us (14%)
  waiting for transfers between devices  2.23 us (4%)
  between operations  0.84 us (2%)
    pallas_call x1, Pallas kernels, work(): pl.pallas_call(sweeps, out_shape=(out, out), in_specs=[VMEM] * 6, out_spe...  17.8 us
    all_gather x1, blocking collectives, swapped(): lax.all_gather(block, ('tm', 'space'), axis_index_groups=pairs(mate_of, s...  16.3 us
    ppermute x2, starting transfers between devices, sent(): return lax.ppermute(block, ('tm', 'space'), route)  7.42 us
    pallas_call x1, Pallas kernels, ready_made(): pl.pallas_call(prepare, out_shape=(jax.ShapeDtypeStruct((FP, 3 * KR), BF)...  3.98 us
    all_gather x1, blocking collectives, per_device(): near = lax.all_gather(jnp.concatenate([close, distant], axis=0), 'tm')  2.69 us
    ppermute x2, waiting for transfers between devices, sent(): return lax.ppermute(block, ('tm', 'space'), route)  2.23 us
    all_gather x1, blocking collectives, per_device(): far = lax.all_gather(across, 'tm')  2.04 us
  transfers between devices with their start and end apart: 2, of which 1 were waited for; matrix products, arithmetic and copies ran while one was open for 0% of the time, Pallas kernels for 7%

profile of v4, /device:TPU:1, one launch (start us, length us, event | category | flops | bytes accessed | tf_op | source)
XLA Modules:
  0.0 53.5 jit_solution(15794450755841502347)
XLA Ops:
  0.6 0.0 copy-start.2
  0.6 0.0 copy-start
  0.7 0.0 copy-start.1
  0.7 16.3 %all_gather.13 = f32[2,320,128]{2,1,0:T(8,128)S(1)} all-gather(f32[1,320,128]{2,1,0:T(8,128)} %param.4), channel_id=1, replica_groups={{0,4},{1,5},{2,6},{3,7},{8,12},{9,13},{10,14},{11,15},{16,20},{17,21},{..., dimensions={0}, use_global_device_ids=true | all-gather | bytes 491520 | tf_op jit(solution)/shard_map/all_gather | solution.py:392
  17.0 2.0 %all_gather.14.far = f32[2,320,128]{2,1,0:T(8,128)S(1)} all-gather(f32[1,320,128]{2,1,0:T(8,128)S(1)} %slice_select_fusion), channel_id=1, replica_groups=mesh['tm'=2,'space'=256] {'tm'}, dimensions={0}, use_global_device_ids=true | all-gather | bytes 491520 | tf_op jit(solution)/shard_map/all_gather | solution.py:427
  19.1 4.7 %collective-permute-start.1 = (f32[320,128]{1,0:T(8,128)S(1)}, f32[320,128]{1,0:T(8,128)S(1)}, u32[]{:S(2)}, u32[]{:S(2)}) collective-permute-start(f32[320,128]{1,0:T(8,128)S(1)} %get-tuple-element.20), channel_id=1, source_target_pairs={{0,2},{2,0},{1,3},{3,1},{4,6},{6,4},{5,7},{7,5},{8,10},{10,8},{9,1... | collective-permute-start | bytes 491528 | tf_op jit(solution)/shard_map/ppermute | solution.py:400
  23.9 2.8 %collective-permute-start = (f32[640,128]{1,0:T(8,128)S(1)}, f32[640,128]{1,0:T(8,128)S(1)}, u32[]{:S(2)}, u32[]{:S(2)}) collective-permute-start(f32[640,128]{1,0:T(8,128)S(1)} %pad_maximum_fusion.1), channel_id=1, source_target_pairs={{0,1},{1,0},{2,3},{3,2},{4,5},{5,4},{6,7},{7,6},{8,9},{9,8},{10,11... | collective-permute-start | bytes 983048 | tf_op jit(solution)/shard_map/ppermute | solution.py:400
  26.6 0.0 copy-done.2
  26.6 0.0 copy-done
  26.7 0.0 copy-done.1
  26.7 4.0 %prepare.1 = (bf16[320,2400]{1,0:T(8,128)(2,1)S(1)}, bf16[320,480]{1,0:T(8,128)(2,1)S(1)}, bf16[320,960]{1,0:T(8,128)(2,1)S(1)}, f32[3,4,320,128]{3,2,1,0:T(8,128)S(1)}, f32[4,320,128]{2,1,0:T(8,128)S(1)}) custom-call(f32[320,128]{1,0:T(8,128)S(1)} %get-tuple-element.21.own, f32[2,320,128]{2,1,0:T(8,128)S(1)} %all_gather.14.far, f32[320,320]{1,0:T(8,128)S(1)} %copy-done.1, ...), custom_call_target="tpu_custom_call" | custom-call | flops 4000000000 | bytes 6000000 | tf_op jit(solution)/shard_map/prepare/pallas_call | solution.py:328
  30.7 0.0 collective-permute-done.1
  30.7 2.2 %collective-permute-done = f32[640,128]{1,0:T(8,128)S(1)} collective-permute-done((f32[640,128]{1,0:T(8,128)S(1)}, f32[640,128]{1,0:T(8,128)S(1)}, u32[]{:S(2)}, u32[]{:S(2)}) %collective-permute-start) | collective-permute-done | bytes 327712 | tf_op jit(solution)/shard_map/ppermute | solution.py:400
  32.9 2.7 %all-gather = f32[1920,128]{1,0:T(8,128)S(1)} all-gather(f32[960,128]{1,0:T(8,128)S(1)} %pad_maximum_fusion), channel_id=2, replica_groups=mesh['tm'=2,'space'=256] {'tm'}, dimensions={0}, use_global_device_ids=true | all-gather | bytes 1474560 | tf_op jit(solution)/shard_map/all_gather | solution.py:437
  35.6 17.8 %sweeps.1 = (f32[2,320,128]{2,1,0:T(8,128)}, f32[2,320,128]{2,1,0:T(8,128)}) custom-call(f32[3,4,320,128]{3,2,1,0:T(8,128)S(1)} %get-tuple-element.9.ready, f32[4,320,128]{2,1,0:T(8,128)S(1)} %get-tuple-element.10.part, f32[2,960,128]{2,1,0:T(8,128)S(1)} %bitcast.17, bf16[320,2400]{1,0:T(8,128)(2,1)S(1)} %get-tuple-element.11.op_r, ...), custom_call_target="tpu_custom_call" | custom-call | tf_op jit(solution)/shard_map/sweeps/pallas_call | solution.py:353
  (5 shorter events, 0.1 us)
Async XLA Ops:
  0.6 26.0 %copy-start.2 = (f32[320,320]{1,0:T(8,128)S(1)}, f32[320,320]{1,0:T(8,128)}, u32[]{:S(2)}) copy-start(f32[320,320]{1,0:T(8,128)} %rate.1) | copy-start | bytes 1228804
  0.6 26.0 %copy-start = (f32[6,320,80]{1,2,0:T(8,128)S(1)}, f32[6,320,80]{1,2,0:T(8,128)}, u32[]{:S(2)}) copy-start(f32[6,320,80]{1,2,0:T(8,128)} %param.6) | copy-start | bytes 1843204
  0.7 26.0 %copy-start.1 = (f32[320,320]{1,0:T(8,128)S(1)}, f32[320,320]{1,0:T(8,128)}, u32[]{:S(2)}) copy-start(f32[320,320]{1,0:T(8,128)} %volume.1) | copy-start | bytes 1228804
  19.1 11.5 %collective-permute-start.1 = (f32[320,128]{1,0:T(8,128)S(1)}, f32[320,128]{1,0:T(8,128)S(1)}, u32[]{:S(2)}, u32[]{:S(2)}) collective-permute-start(f32[320,128]{1,0:T(8,128)S(1)} %get-tuple-element.20), channel_id=1, source_target_pairs={{0,2},{2,0},{1,3},{3,1},{4,6},{6,4},{5,7},{7,5},{8,10},{10,8},{9,1... | collective-permute-start | bytes 491528 | tf_op jit(solution)/shard_map/ppermute | solution.py:400
  23.9 9.0 %collective-permute-start = (f32[640,128]{1,0:T(8,128)S(1)}, f32[640,128]{1,0:T(8,128)S(1)}, u32[]{:S(2)}, u32[]{:S(2)}) collective-permute-start(f32[640,128]{1,0:T(8,128)S(1)} %pad_maximum_fusion.1), channel_id=1, source_target_pairs={{0,1},{1,0},{2,3},{3,2},{4,5},{5,4},{6,7},{7,6},{8,9},{9,8},{10,11... | collective-permute-start | bytes 983048 | tf_op jit(solution)/shard_map/ppermute | solution.py:400

commit v5 on v4

--- a/solution.py
+++ b/solution.py
@@ -142,7 +142,7 @@
         part[s] = y[0, s] + lanes_of(product, s)
 
 
-def sweeps(ready, part, near, op_r, op_x, op_c, starts, ends, y, u1, u2, yp, w, v, b0, b1, b2, b3, bx, bc, bd, up_op, lo_op):
+def sweeps(ready, part, near, op_r, op_x, op_c, starts, ends, y, u1, u2, yp, w, v, b0, b1, b2, b3, b4, b5, b6, b7, bx, bc, bd, up_op, lo_op):
     core, place_here = lax.axis_index("tm"), lax.axis_index("space")
     col, odd_row = lax.rem(place_here, ROW), lax.rem(lax.div(place_here, ROW), 2)
 
@@ -237,15 +237,15 @@
         second(4, None, range(2)),
         second(4, 0, range(2, 4)),
     ]
-    buffers = (b0, b1, b2, b3)
+    buffers = (b0, b1, b2, b3, b4, b5, b6, b7)
     tasks[0][0](b0)
     tasks[1][0](b1)
     for i, (_, run) in enumerate(tasks):
         if i + 2 < len(tasks) and i in (0, 1):
-            tasks[i + 2][0](buffers[(i + 2) % 4])
-        run(buffers[i % 4])
+            tasks[i + 2][0](buffers[(i + 2) % 8])
+        run(buffers[i % 8])
         if i + 2 < len(tasks) and i not in (0, 1):
-            tasks[i + 2][0](buffers[(i + 2) % 4])
+            tasks[i + 2][0](buffers[(i + 2) % 8])
 
     for k in range(5):
         yp[k, 0] = y[k + 2, 0]
@@ -366,6 +366,10 @@
             pltpu.VMEM((3 * KR, NT * EYZ), BF),
             pltpu.VMEM((3 * KR, NT * EYZ), BF),
             pltpu.VMEM((3 * KR, NT * EYZ), BF),
+            pltpu.VMEM((3 * KR, NT * EYZ), BF),
+            pltpu.VMEM((3 * KR, NT * EYZ), BF),
+            pltpu.VMEM((3 * KR, NT * EYZ), BF),
+            pltpu.VMEM((3 * KR, NT * EYZ), BF),
             pltpu.VMEM((6 * FACE, NT * EYZ), BF),
             pltpu.VMEM((3 * FP, 6 * EYZ), BF),
             pltpu.VMEM((2, 3 * FP, 5 * EYZ), BF),

time: 53.6 us -> 53.3 us (level)
  no operation moved by 1% of the time
where the time goes in v5:
time: 53.3 us; the launch traced here: 53.1 us
  Pallas kernels  21.5 us (40%)
  blocking collectives  21 us (39%)
  starting transfers between devices  7.42 us (14%)
  waiting for transfers between devices  2.23 us (4%)
  between operations  0.84 us (2%)
    pallas_call x1, Pallas kernels, work(): pl.pallas_call(sweeps, out_shape=(out, out), in_specs=[VMEM] * 6, out_spe...  17.5 us
    all_gather x1, blocking collectives, swapped(): lax.all_gather(block, ('tm', 'space'), axis_index_groups=pairs(mate_of, s...  16.3 us
    ppermute x2, starting transfers between devices, sent(): return lax.ppermute(block, ('tm', 'space'), route)  7.42 us
    pallas_call x1, Pallas kernels, ready_made(): pl.pallas_call(prepare, out_shape=(jax.ShapeDtypeStruct((FP, 3 * KR), BF)...  3.98 us
    all_gather x1, blocking collectives, per_device(): near = lax.all_gather(jnp.concatenate([close, distant], axis=0), 'tm')  2.69 us
    ppermute x2, waiting for transfers between devices, sent(): return lax.ppermute(block, ('tm', 'space'), route)  2.23 us
    all_gather x1, blocking collectives, per_device(): far = lax.all_gather(across, 'tm')  2.04 us
  transfers between devices with their start and end apart: 2, of which 1 were waited for; matrix products, arithmetic and copies ran while one was open for 0% of the time, Pallas kernels for 7%

profile of v5, /device:TPU:1, one launch (start us, length us, event | category | flops | bytes accessed | tf_op | source)
XLA Modules:
  0.0 53.1 jit_solution(8410004499596740506)
XLA Ops:
  0.6 0.0 copy-start.2
  0.6 0.0 copy-start
  0.7 0.0 copy-start.1
  0.7 16.3 %all_gather.13 = f32[2,320,128]{2,1,0:T(8,128)S(1)} all-gather(f32[1,320,128]{2,1,0:T(8,128)} %param.4), channel_id=1, replica_groups={{0,4},{1,5},{2,6},{3,7},{8,12},{9,13},{10,14},{11,15},{16,20},{17,21},{..., dimensions={0}, use_global_device_ids=true | all-gather | bytes 491520 | tf_op jit(solution)/shard_map/all_gather | solution.py:396
  17.0 2.0 %all_gather.14.far = f32[2,320,128]{2,1,0:T(8,128)S(1)} all-gather(f32[1,320,128]{2,1,0:T(8,128)S(1)} %slice_select_fusion), channel_id=1, replica_groups=mesh['tm'=2,'space'=256] {'tm'}, dimensions={0}, use_global_device_ids=true | all-gather | bytes 491520 | tf_op jit(solution)/shard_map/all_gather | solution.py:431
  19.1 4.7 %collective-permute-start.1 = (f32[320,128]{1,0:T(8,128)S(1)}, f32[320,128]{1,0:T(8,128)S(1)}, u32[]{:S(2)}, u32[]{:S(2)}) collective-permute-start(f32[320,128]{1,0:T(8,128)S(1)} %get-tuple-element.20), channel_id=1, source_target_pairs={{0,2},{2,0},{1,3},{3,1},{4,6},{6,4},{5,7},{7,5},{8,10},{10,8},{9,1... | collective-permute-start | bytes 491528 | tf_op jit(solution)/shard_map/ppermute | solution.py:404
  23.9 2.8 %collective-permute-start = (f32[640,128]{1,0:T(8,128)S(1)}, f32[640,128]{1,0:T(8,128)S(1)}, u32[]{:S(2)}, u32[]{:S(2)}) collective-permute-start(f32[640,128]{1,0:T(8,128)S(1)} %pad_maximum_fusion.1), channel_id=1, source_target_pairs={{0,1},{1,0},{2,3},{3,2},{4,5},{5,4},{6,7},{7,6},{8,9},{9,8},{10,11... | collective-permute-start | bytes 983048 | tf_op jit(solution)/shard_map/ppermute | solution.py:404
  26.6 0.0 copy-done.2
  26.6 0.0 copy-done
  26.7 0.0 copy-done.1
  26.7 4.0 %prepare.1 = (bf16[320,2400]{1,0:T(8,128)(2,1)S(1)}, bf16[320,480]{1,0:T(8,128)(2,1)S(1)}, bf16[320,960]{1,0:T(8,128)(2,1)S(1)}, f32[3,4,320,128]{3,2,1,0:T(8,128)S(1)}, f32[4,320,128]{2,1,0:T(8,128)S(1)}) custom-call(f32[320,128]{1,0:T(8,128)S(1)} %get-tuple-element.21.own, f32[2,320,128]{2,1,0:T(8,128)S(1)} %all_gather.14.far, f32[320,320]{1,0:T(8,128)S(1)} %copy-done.1, ...), custom_call_target="tpu_custom_call" | custom-call | flops 4000000000 | bytes 6000000 | tf_op jit(solution)/shard_map/prepare/pallas_call | solution.py:328
  30.7 0.0 collective-permute-done.1
  30.7 2.2 %collective-permute-done = f32[640,128]{1,0:T(8,128)S(1)} collective-permute-done((f32[640,128]{1,0:T(8,128)S(1)}, f32[640,128]{1,0:T(8,128)S(1)}, u32[]{:S(2)}, u32[]{:S(2)}) %collective-permute-start) | collective-permute-done | bytes 327712 | tf_op jit(solution)/shard_map/ppermute | solution.py:404
  32.9 2.7 %all-gather = f32[1920,128]{1,0:T(8,128)S(1)} all-gather(f32[960,128]{1,0:T(8,128)S(1)} %pad_maximum_fusion), channel_id=2, replica_groups=mesh['tm'=2,'space'=256] {'tm'}, dimensions={0}, use_global_device_ids=true | all-gather | bytes 1474560 | tf_op jit(solution)/shard_map/all_gather | solution.py:441
  35.6 17.5 %sweeps.1 = (f32[2,320,128]{2,1,0:T(8,128)}, f32[2,320,128]{2,1,0:T(8,128)}) custom-call(f32[3,4,320,128]{3,2,1,0:T(8,128)S(1)} %get-tuple-element.9.ready, f32[4,320,128]{2,1,0:T(8,128)S(1)} %get-tuple-element.10.part, f32[2,960,128]{2,1,0:T(8,128)S(1)} %bitcast.17, bf16[320,2400]{1,0:T(8,128)(2,1)S(1)} %get-tuple-element.11.op_r, ...), custom_call_target="tpu_custom_call" | custom-call | tf_op jit(solution)/shard_map/sweeps/pallas_call | solution.py:353
  (5 shorter events, 0.1 us)
Async XLA Ops:
  0.6 26.0 %copy-start.2 = (f32[320,320]{1,0:T(8,128)S(1)}, f32[320,320]{1,0:T(8,128)}, u32[]{:S(2)}) copy-start(f32[320,320]{1,0:T(8,128)} %rate.1) | copy-start | bytes 1228804
  0.6 26.0 %copy-start = (f32[6,320,80]{1,2,0:T(8,128)S(1)}, f32[6,320,80]{1,2,0:T(8,128)}, u32[]{:S(2)}) copy-start(f32[6,320,80]{1,2,0:T(8,128)} %param.6) | copy-start | bytes 1843204
  0.7 26.0 %copy-start.1 = (f32[320,320]{1,0:T(8,128)S(1)}, f32[320,320]{1,0:T(8,128)}, u32[]{:S(2)}) copy-start(f32[320,320]{1,0:T(8,128)} %volume.1) | copy-start | bytes 1228804
  19.1 11.5 %collective-permute-start.1 = (f32[320,128]{1,0:T(8,128)S(1)}, f32[320,128]{1,0:T(8,128)S(1)}, u32[]{:S(2)}, u32[]{:S(2)}) collective-permute-start(f32[320,128]{1,0:T(8,128)S(1)} %get-tuple-element.20), channel_id=1, source_target_pairs={{0,2},{2,0},{1,3},{3,1},{4,6},{6,4},{5,7},{7,5},{8,10},{10,8},{9,1... | collective-permute-start | bytes 491528 | tf_op jit(solution)/shard_map/ppermute | solution.py:404
  23.9 9.0 %collective-permute-start = (f32[640,128]{1,0:T(8,128)S(1)}, f32[640,128]{1,0:T(8,128)S(1)}, u32[]{:S(2)}, u32[]{:S(2)}) collective-permute-start(f32[640,128]{1,0:T(8,128)S(1)} %pad_maximum_fusion.1), channel_id=1, source_target_pairs={{0,1},{1,0},{2,3},{3,2},{4,5},{5,4},{6,7},{7,6},{8,9},{9,8},{10,11... | collective-permute-start | bytes 983048 | tf_op jit(solution)/shard_map/ppermute | solution.py:404
